TPU v7x, 512 devices: a whole 4x8x8 slice. The times are simulated.
512 devices in a mesh: wide: 64 (over z_lo, x, y), narrow: 8 (over z_hi, core).
Axes of the slice: x: 4, y: 8, z: 8 (z_hi: 4, z_lo: 2; z = z_hi * 2 + z_lo), core: 2. Of those that a mesh axis runs over, the one named last changes fastest.
Arguments:
- users: bfloat16 [65536, 128], P('wide'), may hold values from -12 to 12
- items: bfloat16 [65536, 128], P(('wide', 'narrow')), may hold values from -12 to 12
- item_scale: bfloat16 [65536], P(('wide', 'narrow')), may hold values from 0.25 to 4
- user_mass: float32 [65536], P('wide'), may hold values from 0.5 to 2
- item_mass: float32 [65536], P(('wide', 'narrow')), may hold values from 0.5 to 2
Outputs:
- user_scale: float32 [65536], P('wide')
- item_scale_new: float32 [65536], P(('wide', 'narrow'))
All inputs are finite; a program needn't handle non-finite values.
Results may differ from a plain program's by a relative error of at most 0.0003.
Values may be sent and summed in bfloat16 or wider, within the bound.
A program may use at most 64 MiB of HBM per device.

v0:
```python
import math

import jax
import jax.numpy as jnp
from jax import lax
from jax.sharding import PartitionSpec as P


def unit_rows(rows):
    values = rows.astype(jnp.float32)
    squares = jnp.sum(values * values, axis=1, keepdims=True) + 1e-06
    return (values * lax.rsqrt(squares)).astype(jnp.bfloat16)


def kernel_block(user_hat, item_block):
    scores = lax.dot_general(
        user_hat, item_block, (((1,), (1,)), ((), ())), preferred_element_type=jnp.float32
    )
    return jnp.exp(scores / 0.5)


def row_terms(user_hat, item_rows, item_weights):
    count = item_rows.shape[0]
    block = math.gcd(count, 1024)
    stacked = item_rows.reshape(count // block, block, item_rows.shape[1])
    weights = item_weights.reshape(count // block, block)

    def row_step(total, pair):
        kernel = kernel_block(user_hat, pair[0])
        return (
            total + jnp.dot(kernel, pair[1].astype(jnp.float32), precision=lax.Precision.HIGHEST),
            None,
        )

    total, unused = lax.scan(
        row_step, jnp.zeros((user_hat.shape[0],), jnp.float32), (stacked, weights)
    )
    return total


def column_terms(user_hat, scale, item_rows):
    count = item_rows.shape[0]
    block = math.gcd(count, 1024)
    stacked = item_rows.reshape(count // block, block, item_rows.shape[1])

    def column_step(carry, piece):
        kernel = kernel_block(user_hat, piece)
        return (carry, jnp.dot(scale, kernel, precision=lax.Precision.HIGHEST))

    unused, sums = lax.scan(column_step, 0.0, stacked)
    return sums.reshape(count)


def on_device(users, items, item_scale, user_mass, item_mass):
    user_hat = unit_rows(users)
    item_hat = unit_rows(items)
    item_count = items.shape[0] * lax.axis_size("wide") * lax.axis_size("narrow")
    user_count = users.shape[0] * lax.axis_size("wide")
    held_rows, held_weights = (
        lax.all_gather(item_hat, "wide", axis=0, tiled=True),
        lax.all_gather(item_scale, "wide", axis=0, tiled=True),
    )
    partial_value = row_terms(user_hat, held_rows, held_weights)
    row_total = lax.psum(partial_value, "narrow")
    user_scale = user_mass / (row_total / item_count)
    column_total = lax.psum_scatter(
        column_terms(user_hat, user_scale, held_rows), "wide", scatter_dimension=0, tiled=True
    )
    item_scale_new = item_mass / (column_total / user_count)
    return (user_scale, item_scale_new)


def solution(mesh):
    in_specs = (
        P("wide", None),
        P(("wide", "narrow"), None),
        P(("wide", "narrow")),
        P("wide"),
        P(("wide", "narrow")),
    )
    out_specs = (P("wide"), P(("wide", "narrow")))
    return jax.shard_map(
        on_device, mesh=mesh, in_specs=in_specs, out_specs=out_specs, check_vma=False
    )
```

profile of v0, /device:TPU:64, one launch (start us, length us, event | category | flops | bytes accessed | tf_op | source)
XLA Modules:
  0.0 719.3 jit_solution(5562536470229533462)
XLA Ops:
  7.2 0.0 all-gather.3.cloned.1.call-start
  7.2 0.9 fusion.25
  8.1 1.5 fusion.26
  9.5 0.0 all-gather.3.cloned.1.call-update
  9.6 154.0 %all-gather = bf16[64,1,128]{2,1,0:T(2,128)(2,1)S(1)} all-gather(bf16[1,1,128]{2,1,0:T(2,128)(2,1)} %bitcast.53), channel_id=1, replica_groups=mesh['wide'=64,'narrow'=8] {'wide'}, dimensions={0}, use_global_device_ids=true | all-gather | bytes 16640 | tf_op jit(solution)/shard_map/all_gather | solution.py:61
  163.6 0.1 reduce
  163.7 1.3 dynamic-slice
  165.6 1.2 fusion.23
  166.8 1.2 fusion.24
  167.9 147.5 %all-gather.3.cloned.1.call-done = bf16[8192,128]{1,0:T(8,128)(2,1)} async-done(((bf16[128,128]{1,0:T(8,128)(2,1)}), bf16[8192,128]{1,0:T(8,128)(2,1)}) %all-gather.3.cloned.1.call-update) | async-done | bytes 2097168 | tf_op jit(solution)/shard_map/all_gather | solution.py:60
  315.4 0.0 copy-start.1
  315.4 28.1 %while.22 = (s32[]{:T(128)}, f32[1024]{0:T(1024)S(1)}, bf16[8,1024,128]{2,1,0:T(8,128)(2,1)}, bf16[1024,128]{1,0:T(8,128)(2,1)S(1)}, bf16[8,1024]{1,0:T(8,128)(2,1)S(1)}, /*index=5*/s32[]{:T(128)}, s32[]{:T(128)}) while((s32[]{:T(128)}, f32[1024]{0:T(1024)S(1)}, bf16[8,1024,128]{2,1,0:T(8,128)(2,1)}, ...), condition=%wide.region_3.4_spmd.clone, body=%wide.region_2.3_spmd.clone.sunk | while | flops 282068992 | bytes 8933979 | solution.py:35
  315.4 1.7 fusion.53
  317.0 1.8 fusion.54
  318.9 1.7 fusion.53
  320.6 1.8 fusion.54
  322.4 1.7 fusion.53
  324.1 1.8 fusion.54
  325.9 1.7 fusion.53
  327.6 1.8 fusion.54
  329.4 1.7 fusion.53
  331.1 1.8 fusion.54
  333.0 1.7 fusion.53
  334.6 1.8 fusion.54
  336.5 1.7 fusion.53
  338.1 1.8 fusion.54
  340.0 1.7 fusion.53
  341.7 1.8 fusion.54
  343.5 14.5 %psum.7 = f32[1024]{0:T(1024)S(1)} all-reduce(f32[1024]{0:T(1024)S(1)} %get-tuple-element.56), channel_id=1, replica_groups=mesh['wide'=64,'narrow'=8] {'narrow'}, use_global_device_ids=true, to_apply=%region_4.5 | all-reduce | flops 1024 | bytes 8192 | tf_op jit(solution)/shard_map/psum | solution.py:64
  358.0 0.0 copy-done.1
  358.0 0.0 copy-start.2
  358.0 46.1 %while.21 = (s32[]{:T(128)}, f32[8,1024]{1,0:T(8,128)S(1)}, bf16[8,1024,128]{2,1,0:T(8,128)(2,1)}, bf16[1024,128]{1,0:T(8,128)(2,1)S(1)}, f32[1024]{0:T(1024)S(1)}, /*index=5*/s32[]{:T(128)}, s32[]{:T(128)}) while((s32[]{:T(128)}, f32[8,1024]{1,0:T(8,128)S(1)}, bf16[8,1024,128]{2,1,0:T(8,128)(2,1)}, bf16[1024,128]{1,0:T(8,128)(2,1)S(1)}, ...), condition=%wide.region_6.7_spmd, body=%wide.region_5.6_spmd.sunk | while | flops 282066944 | bytes 8929873 | solution.py:50
  358.1 1.7 fusion.47
  359.7 4.0 fusion.48
  363.7 0.1 dynamic_update_slice.5
  363.8 1.7 fusion.47
  365.5 4.0 fusion.48
  369.5 0.1 dynamic_update_slice.5
  369.6 1.7 fusion.47
  371.2 4.0 fusion.48
  375.2 0.1 dynamic_update_slice.5
  375.3 1.7 fusion.47
  377.0 4.0 fusion.48
  381.0 0.1 dynamic_update_slice.5
  381.1 1.7 fusion.47
  382.8 4.0 fusion.48
  386.7 0.1 dynamic_update_slice.5
  386.9 1.7 fusion.47
  388.5 4.0 fusion.48
  392.5 0.1 dynamic_update_slice.5
  392.6 1.7 fusion.47
  394.3 4.0 fusion.48
  398.3 0.1 dynamic_update_slice.5
  398.4 1.7 fusion.47
  400.1 4.0 fusion.48
  404.0 0.1 dynamic_update_slice.5
  404.1 0.0 copy-start
  404.2 307.7 %all-reduce = f32[8192]{0:T(1024)S(1)} all-reduce(f32[8192]{0:T(1024)S(1)} %bitcast.51), channel_id=2, replica_groups=mesh['wide'=64,'narrow'=8] {'wide'}, use_global_device_ids=true, to_apply=%region_7.8.clone | all-reduce | flops 8192 | bytes 65536
  711.9 0.0 copy-done.2
  711.9 0.6 fusion.27
  712.4 0.0 copy-done
  (15 shorter events, 0.1 us)
Async XLA Ops:
  7.2 308.2 %all-gather.3.cloned.1.call-start = ((), (), s32[]{:S(2)}) async-start(), calls=%async_computation | async-start | bytes 2129920 | tf_op jit(solution)/shard_map/all_gather | solution.py:60
  315.4 42.6 %copy-start.1 = (f32[1024]{0:T(1024)S(1)}, f32[1024]{0:T(1024)}, u32[]{:S(2)}) copy-start(f32[1024]{0:T(1024)} %param.12) | copy-start | bytes 12292
  358.0 353.8 %copy-start.2 = (f32[128]{0:T(128)S(1)}, f32[128]{0:T(128)}, u32[]{:S(2)}) copy-start(f32[128]{0:T(128)} %param.13) | copy-start | bytes 1540
  404.1 308.3 %copy-start = (f32[1024]{0:T(1024)}, f32[1024]{0:T(1024)S(1)}, u32[]{:S(2)}) copy-start(f32[1024]{0:T(1024)S(1)} %get-tuple-element.204) | copy-start | bytes 12292
Sparse Core Ops, SparseCore 0:
  10.1 305.2 all-gather.2
where the time goes:
time: 720 us; the launch traced here: 719 us
  blocking collectives  476 us (66%)
  waiting for transfers between devices  147 us (20%)
  matrix products  73.1 us (10%)
  between operations  14.8 us (2%)
    unnamed x1, blocking collectives  308 us
    all_gather x1, blocking collectives, on_device(): lax.all_gather(item_scale, 'wide', axis=0, tiled=True)  154 us
    all_gather x1, waiting for transfers between devices, on_device(): lax.all_gather(item_hat, 'wide', axis=0, tiled=True)  147 us
    dot_general x8, matrix products, column_step(): return (carry, jnp.dot(scale, kernel, precision=lax.Precision.HIGHEST))  31.8 us
    dot_general x16, matrix products, kernel_block(): lax.dot_general(user_hat, item_block, (((1,), (1,)), ((), ())), preferred...  26.5 us
    dot_general x8, matrix products, row_step(): jnp.dot(kernel, pair[1].astype(jnp.float32), precision=lax.Precision.HIGH...  14.7 us
    psum x1, blocking collectives, on_device(): row_total = lax.psum(partial_value, 'narrow')  14.5 us
  transfers between devices with their start and end apart: 1, of which 1 were waited for; matrix products, arithmetic and copies ran while one was open for 1% of the time, Pallas kernels for 0%

commit v1 on v0

v1 whole, which is shorter than its diff:
```python
import functools
import math

import jax
import jax.numpy as jnp
from jax import lax
from jax.experimental import pallas as pl
from jax.experimental.pallas import tpu as pltpu
from jax.sharding import PartitionSpec as P

MESH = pl.DeviceIdType.MESH
F32 = jnp.float32
BF16 = jnp.bfloat16

NX, NY, NZ = 4, 8, 8
BLOCK = 128
HALF = 64
CHUNK = NX * BLOCK
USERS = 1024
TILE = 512
TILES = 2 * USERS // TILE
WIDTH = 128
SCALE = 2.0 * math.log2(math.e)


def unit_rows(values, axis):
    squares = jnp.sum(values * values, axis=axis, keepdims=True) + 1e-06
    return (values * lax.rsqrt(squares)).astype(BF16)


def body(
    item_count, user_count,
    users_ref, items_ref, weight_ref, user_mass_ref, item_mass_ref,
    user_scale_ref, item_scale_ref,
    rows, weights, bias, users, kernel, row_acc, row_parts, masses, user_rows, column_send,
    column_y, column_x,
    x_send, x_recv, y_send, y_recv, w_send, w_recv, u_send, u_recv, r_send, r_recv,
    cy_send, cy_recv, cx_send, cx_recv,
):
    wide = lax.axis_index("wide")
    narrow = lax.axis_index("narrow")
    z_lo, x, y = wide // (NX * NY), (wide // NY) % NX, wide % NY
    z_hi, core = narrow // 2, narrow % 2
    z = z_hi * 2 + z_lo
    line = z * 2 + core

    def plane(px, py):
        return (z_lo * (NX * NY) + px * NY + py, narrow)

    def column(pline):
        pz, pc = pline // 2, pline % 2
        return ((pz % 2) * (NX * NY) + x * NY + y, (pz // 2) * 2 + pc)

    def at_x(step):
        return plane((x + step) % NX, y)

    def at_y(step):
        return plane(x, (y + step) % NY)

    def at_line(step):
        return column((line + step) % (2 * NZ))

    barrier = pltpu.get_barrier_semaphore()

    def greet(partner):
        pl.semaphore_signal(barrier, inc=1, device_id=partner, device_id_type=MESH)

    def greet_x(step, carry):
        greet(at_x(step))
        return carry

    def greet_y(step, carry):
        greet(at_y(step))
        return carry

    def greet_line(step, carry):
        greet(at_line(step))
        return carry

    lax.fori_loop(1, NX, greet_x, 0)
    lax.fori_loop(1, NY, greet_y, 0)
    lax.fori_loop(1, 2 * NZ, greet_line, 0)

    hat = unit_rows(items_ref[...].astype(F32), 1)
    rows[y, 0, x] = hat[:HALF]
    rows[y, 1, x] = hat[HALF:]
    weights[y, x] = weight_ref[...].astype(F32)

    pl.semaphore_wait(barrier, NX - 1 + NY - 1 + 2 * NZ - 1)

    def remote(src, dst, send, recv, partner):
        return pltpu.make_async_remote_copy(
            src_ref=src, dst_ref=dst, send_sem=send, recv_sem=recv,
            device_id=partner, device_id_type=MESH,
        )

    def x_copies(step):
        source = (x - step) % NX
        out, back = [], []
        for half in (0, 1):
            out.append(remote(rows.at[y, half, x], rows.at[y, half, x],
                              x_send.at[step, half], x_recv.at[step, half], at_x(step)))
            back.append(remote(rows.at[y, half, source], rows.at[y, half, source],
                               x_send.at[step, half], x_recv.at[step, half], at_x(step)))
        out.append(remote(weights.at[y, x], weights.at[y, x],
                          x_send.at[step, 2], x_recv.at[step, 2], at_x(step)))
        back.append(remote(weights.at[y, source], weights.at[y, source],
                           x_send.at[step, 2], x_recv.at[step, 2], at_x(step)))
        return out, back

    for step in (1, 3, 2):
        for copy in x_copies(step)[0]:
            copy.start()

    ones = (lax.broadcasted_iota(jnp.int32, (WIDTH, TILE), 0) < 12).astype(F32).astype(BF16)
    for half in (0, 1):
        values = users_ref[half * TILE:(half + 1) * TILE, :].astype(F32).T
        users[z_lo * 2 + half, 0:WIDTH, :] = unit_rows(values, 0)
    for tile in range(TILES):
        users[tile, WIDTH:2 * WIDTH, :] = ones
    masses[z_lo] = user_mass_ref[...]

    z_up, z_down = at_line(2), at_line(2 * NZ - 2)

    def u_copies(block):
        out = []
        for half, partner in ((0, z_up), (1, z_down)):
            part = users.at[block * 2 + half, 0:WIDTH, :]
            out.append(remote(part, part, u_send.at[half], u_recv.at[half], partner))
        out.append(remote(masses.at[block], masses.at[block], u_send.at[2], u_recv.at[2], z_up))
        return out

    for copy in u_copies(z_lo):
        copy.start()

    for step in range(1, NX):
        for copy in x_copies(step)[1]:
            copy.wait_recv()

    def y_half(way, hop, source, half):
        part = rows.at[source, half]
        return remote(part, part, y_send.at[way, hop, half], y_recv.at[way, hop, half],
                      at_y(1 if way == 0 else NY - 1))

    def w_copy(source, step):
        part = weights.at[source]
        return remote(part, part, w_send.at[step], w_recv.at[step], at_y(step))

    for half in (0, 1):
        for way in (0, 1):
            y_half(way, 1, y, half).start()

    def send_weights(step, carry):
        w_copy(y, step).start()
        return carry

    lax.fori_loop(1, NY, send_weights, 0)

    row_acc[...] = jnp.zeros_like(row_acc)
    lane = lax.broadcasted_iota(jnp.int32, (BLOCK, BLOCK), 1)
    sub = lax.broadcasted_iota(jnp.int32, (8, BLOCK), 0)

    def make_bias(chunk):
        first = jnp.zeros((8, BLOCK), F32)
        second = jnp.zeros((8, BLOCK), F32)
        for block in range(NX):
            value = jnp.broadcast_to(0.5 * jnp.log(weights[chunk, block]), (8, BLOCK))
            high = value.astype(BF16).astype(F32)
            middle = (value - high).astype(BF16).astype(F32)
            low = value - high - middle
            first = jnp.where(sub == block, high, first)
            first = jnp.where(sub == block + 4, middle, first)
            second = jnp.where(sub == block, low, second)
        stacked = jnp.concatenate([first, second, jnp.zeros((BLOCK - 16, BLOCK), F32)], axis=0)
        turned = stacked.T
        for block in range(NX):
            own = jnp.where(lane % 4 == block, turned, 0.0).astype(BF16)
            bias[0, block] = own[:HALF]
            bias[1, block] = own[HALF:]

    def compute(chunk, first, last):
        def tile_step(tile, carry):
            left = jnp.concatenate(
                [rows[chunk].reshape(CHUNK, WIDTH), bias[...].reshape(CHUNK, WIDTH)], axis=1
            )
            scores = jnp.dot(left, users[tile], preferred_element_type=F32)
            values = jnp.exp2(scores * SCALE)
            kernel[chunk, tile] = values
            row_acc[tile] += jnp.sum(values.reshape(CHUNK // 8, 8, TILE), axis=0)
            return carry

        lax.fori_loop(first, last, tile_step, 0)

    make_bias(y)
    compute(y, z_lo * 2, z_lo * 2 + 2)
    for copy in u_copies(1 - z_lo):
        copy.wait_recv()
    compute(y, 2 - z_lo * 2, 4 - z_lo * 2)

    for hop in (1, 2, 3):
        behind, ahead = (y - hop) % NY, (y + hop) % NY
        for half in (0, 1):
            y_half(0, hop, behind, half).wait_recv()
            if hop < 3 or half == 0:
                y_half(0, hop + 1, behind, half).start()
            y_half(1, hop, ahead, half).wait_recv()
            if hop < 3 or half == 1:
                y_half(1, hop + 1, ahead, half).start()
        for source, step in ((behind, hop), (ahead, NY - hop)):
            w_copy(source, step).wait_recv()
            make_bias(source)
            compute(source, 0, TILES)
    far = (y + 4) % NY
    y_half(0, 4, far, 0).wait_recv()
    y_half(1, 4, far, 1).wait_recv()
    w_copy(far, 4).wait_recv()
    make_bias(far)
    compute(far, 0, TILES)

    for tile in range(TILES):
        total = jnp.sum(row_acc[tile], axis=0, keepdims=True)
        for part in range(TILE // 128):
            at = tile * (TILE // 128) + part
            row_parts[line, at:at + 1, :] = total[:, part * 128:(part + 1) * 128]

    def r_copy(source, step):
        part = row_parts.at[source]
        return remote(part, part, r_send.at[step], r_recv.at[step], at_line(step))

    def send_rows(step, carry):
        r_copy(line, step).start()
        return carry

    def wait_rows(step, carry):
        r_copy((line - step) % (2 * NZ), step).wait_recv()
        return carry

    lax.fori_loop(1, 2 * NZ, send_rows, 0)
    lax.fori_loop(1, 2 * NZ, wait_rows, 0)
    total = row_parts[0]
    for part in range(1, 2 * NZ):
        total = total + row_parts[part]
    scale = masses[...].reshape(16, 128) / (total / item_count)
    user_rows[...] = scale.reshape(2, 8, 128)
    user_scale_ref[...] = user_rows[z_lo]

    all_ones = jnp.ones((2 * WIDTH, WIDTH), BF16)
    diagonal = lax.broadcasted_iota(jnp.int32, (HALF, BLOCK), 0)
    across = lax.broadcasted_iota(jnp.int32, (HALF, BLOCK), 1)

    def cy_copy(source, target, step):
        return remote(column_send.at[target], column_y.at[source],
                      cy_send.at[step], cy_recv.at[step], at_y(step))

    def sum_columns(chunk):
        def block_step(block, carry):
            out = jnp.zeros((1, BLOCK), F32)
            for half in (0, 1):
                start = pl.multiple_of(half * (NX * HALF) + block * HALF, HALF)
                acc = jnp.zeros((HALF, 128), F32)
                for tile in range(TILES):
                    for part in range(TILE // 128):
                        at = tile * (TILE // 128) + part
                        scale_row = user_rows[at // 8, at % 8:at % 8 + 1, :]
                        piece = kernel[chunk, tile, pl.ds(start, HALF), part * 128:(part + 1) * 128]
                        acc = acc + piece * scale_row
                high = acc.astype(BF16)
                low = (acc - high.astype(F32)).astype(BF16)
                sums = jnp.dot(jnp.concatenate([high, low], axis=1), all_ones,
                               preferred_element_type=F32)
                kept = jnp.where(across == diagonal + half * HALF, sums, 0.0)
                out = out + jnp.sum(kept, axis=0, keepdims=True)
            column_send[chunk, block] = out
            return carry

        lax.fori_loop(0, NX, block_step, 0)

    def column_step(step, carry):
        target = (y + step) % NY
        sum_columns(target)

        @pl.when(step < NY)
        def _():
            cy_copy(y, target, step).start()

        return carry

    lax.fori_loop(1, NY + 1, column_step, 0)
    column_y[y] = column_send[y]

    def wait_y(step, carry):
        cy_copy((y - step) % NY, y, step).wait_recv()
        return carry

    lax.fori_loop(1, NY, wait_y, 0)
    total = column_y[0]
    for part in range(1, NY):
        total = total + column_y[part]
    column_x[NX] = total

    def cx_copy(source, target, step):
        return remote(column_x.at[NX, target], column_x.at[source, 0],
                      cx_send.at[step], cx_recv.at[step], at_x(step))

    for step in (1, 3, 2):
        cx_copy(x, (x + step) % NX, step).start()
    column_x[x, 0] = column_x[NX, x]
    for step in (1, 3, 2):
        cx_copy((x - step) % NX, x, step).wait_recv()
    total = column_x[0, 0]
    for part in range(1, NX):
        total = total + column_x[part, 0]
    item_scale_ref[...] = item_mass_ref[...] * weights[y, x] / (total / user_count)

    for step in range(1, NX):
        for copy in x_copies(step)[0]:
            copy.wait_send()
        cx_copy(x, (x + step) % NX, step).wait_send()
    for copy in u_copies(z_lo):
        copy.wait_send()
    for hop in (1, 2, 3, 4):
        behind, ahead = (y - hop + 1) % NY, (y + hop - 1) % NY
        for half in (0, 1):
            if hop < 4 or half == 0:
                y_half(0, hop, behind, half).wait_send()
            if hop < 4 or half == 1:
                y_half(1, hop, ahead, half).wait_send()

    def sent_y(step, carry):
        w_copy(y, step).wait_send()
        cy_copy(y, (y + step) % NY, step).wait_send()
        return carry

    def sent_rows(step, carry):
        r_copy(line, step).wait_send()
        return carry

    lax.fori_loop(1, NY, sent_y, 0)
    lax.fori_loop(1, 2 * NZ, sent_rows, 0)


def on_device(users, items, item_scale, user_mass, item_mass):
    user_count = users.shape[0] * lax.axis_size("wide")
    item_count = items.shape[0] * lax.axis_size("wide") * lax.axis_size("narrow")
    dma = pltpu.SemaphoreType.DMA
    vmem = pl.BlockSpec(memory_space=pltpu.VMEM)
    user_scale, item_scale_new = pl.pallas_call(
        functools.partial(body, item_count, user_count),
        out_shape=(
            jax.ShapeDtypeStruct((8, 128), F32),
            jax.ShapeDtypeStruct((1, 128), F32),
        ),
        in_specs=[vmem] * 5,
        out_specs=(vmem, vmem),
        scratch_shapes=[
            pltpu.VMEM((NY, 2, NX, HALF, WIDTH), BF16),
            pltpu.VMEM((NY, NX, 1, BLOCK), F32),
            pltpu.VMEM((2, NX, HALF, BLOCK), BF16),
            pltpu.VMEM((TILES, 2 * WIDTH, TILE), BF16),
            pltpu.VMEM((NY, TILES, CHUNK, TILE), F32),
            pltpu.VMEM((TILES, 8, TILE), F32),
            pltpu.VMEM((2 * NZ, 16, 128), F32),
            pltpu.VMEM((2, 8, 128), F32),
            pltpu.VMEM((2, 8, 128), F32),
            pltpu.VMEM((NY, NX, 1, BLOCK), F32),
            pltpu.VMEM((NY, NX, 1, BLOCK), F32),
            pltpu.VMEM((NX + 1, NX, 1, BLOCK), F32),
            dma((NX, 3)), dma((NX, 3)),
            dma((2, 5, 2)), dma((2, 5, 2)),
            dma((NY,)), dma((NY,)),
            dma((3,)), dma((3,)),
            dma((2 * NZ,)), dma((2 * NZ,)),
            dma((NY,)), dma((NY,)),
            dma((NX,)), dma((NX,)),
        ],
        compiler_params=pltpu.CompilerParams(
            collective_id=0, has_side_effects=True, vmem_limit_bytes=56 * 1024 * 1024
        ),
        cost_estimate=pl.CostEstimate(
            flops=2 * 4096 * 2048 * 256, bytes_accessed=1 << 20, transcendentals=4096 * 2048
        ),
        name="scaling",
    )(
        users,
        items,
        item_scale.reshape(1, 128),
        user_mass.reshape(8, 128),
        item_mass.reshape(1, 128),
    )
    return user_scale.reshape(1024), item_scale_new.reshape(128)


def solution(mesh):
    in_specs = (
        P("wide", None),
        P(("wide", "narrow"), None),
        P(("wide", "narrow")),
        P("wide"),
        P(("wide", "narrow")),
    )
    out_specs = (P("wide"), P(("wide", "narrow")))
    return jax.shard_map(
        on_device, mesh=mesh, in_specs=in_specs, out_specs=out_specs, check_vma=False
    )
```

time: 720 us -> 58.3 us (0.08)
  the two profiles are of different devices: /device:TPU:64 before, /device:TPU:1 now
where the time goes in v1:
time: 58.3 us; the launch traced here: 57.9 us
  Pallas kernels  55.4 us (95%)
  local copies, waits for them, and re-layouts  1.82 us (3%)
  between operations  0.65 us (1%)
    pallas_call x1, Pallas kernels, on_device(): pl.pallas_call(functools.partial(body, item_count, user_count), out_shape...  55.4 us
    unnamed x6, local copies, waits for them, and re-layouts  1.82 us

profile of v1, /device:TPU:1, one launch (start us, length us, event | category | flops | bytes accessed | tf_op | source)
XLA Modules:
  0.0 57.9 jit_solution(819225043158602173)
XLA Ops:
  0.6 55.4 %scaling.1 = (f32[8,128]{1,0:T(8,128)}, f32[1,128]{1,0:T(1,128)}) custom-call(bf16[1024,128]{1,0:T(8,128)(2,1)} %users_ref.1, bf16[128,128]{1,0:T(8,128)(2,1)} %items_ref.1, bf16[1,128]{1,0:T(2,128)(2,1)} %bitcast.7, f32[8,128]{1,0:T(8,128)} %bitcast.6, f32[1,128]{1,0:T(1,128)} %bitcast.8), custom_call_target="tpu_custom_call" | custom-call | flops 4294967296 | bytes 1048576 | tf_op jit(solution)/shard_map/scaling/pallas_call | solution.py:347
  56.0 0.0 copy-start
  56.0 0.7 %copy-done = f32[8,128]{1,0:T(8,128)S(1)} copy-done((f32[8,128]{1,0:T(8,128)S(1)}, f32[8,128]{1,0:T(8,128)}, u32[]{:S(2)}) %copy-start) | copy-done | bytes 4120
  56.7 0.0 copy-start.1
  56.7 0.6 %copy.9 = f32[1024]{0:T(1024)} copy(f32[1024]{0:T(1024)S(1)} %bitcast.5) | data formatting | bytes 8192
  57.3 0.0 copy-done.1
  57.4 0.5 copy.10
Async XLA Ops:
  56.0 0.7 %copy-start = (f32[8,128]{1,0:T(8,128)S(1)}, f32[8,128]{1,0:T(8,128)}, u32[]{:S(2)}) copy-start(f32[8,128]{1,0:T(8,128)} %get-tuple-element.4) | copy-start | bytes 12292
  56.7 0.6 %copy-start.1 = (f32[1,128]{1,0:T(1,128)S(1)}, f32[1,128]{1,0:T(1,128)}, u32[]{:S(2)}) copy-start(f32[1,128]{1,0:T(1,128)} %get-tuple-element.5) | copy-start | bytes 1540

commit v2 on v0

v2 whole, which is shorter than its diff:
```python
import functools
import math

import jax
import jax.numpy as jnp
from jax import lax
from jax.experimental import pallas as pl
from jax.experimental.pallas import tpu as pltpu
from jax.sharding import PartitionSpec as P

MESH = pl.DeviceIdType.MESH
F32 = jnp.float32
BF16 = jnp.bfloat16

NX, NY, NZ = 4, 8, 8
LINE = 2 * NZ
BLOCK = 128
HALF = 64
USERS = 1024
TILE = 512
TILES = 2 * USERS // TILE
PARTS = TILE // 128
WIDTH = 128
SCALE = 2.0 * math.log2(math.e)


def unit_rows(values, axis):
    squares = jnp.sum(values * values, axis=axis, keepdims=True) + 1e-06
    return (values * lax.rsqrt(squares)).astype(BF16)


def three_pieces(weight):
    value = 0.5 * jnp.log(weight)
    high = value.astype(BF16).astype(F32)
    middle = (value - high).astype(BF16).astype(F32)
    return high, middle, value - high - middle


def body(
    item_count,
    users_hbm, items_hbm, weight_hbm, mass_hbm,
    row_total_ref, column_total_ref,
    users_in, items_in, weight_in, rows, turned, users, kernel, row_acc, row_parts, masses,
    user_rows, column_send, column_y, column_x, column_half,
    in_sem, x_send, x_recv, y_send, y_recv, u_send, u_recv, r_send, r_recv,
    cy_send, cy_recv, cx_send, cx_recv,
):
    wide = lax.axis_index("wide")
    narrow = lax.axis_index("narrow")
    y = wide & (NY - 1)
    x = (wide >> 3) & (NX - 1)
    z_lo = wide >> 5
    line = ((narrow >> 1) << 2) | (z_lo << 1) | (narrow & 1)
    wide_no_y = wide - y
    wide_no_x = wide - (x << 3)
    wide_no_z = wide & (NX * NY - 1)

    def at_x(step):
        return (wide_no_x + (((x + step) & (NX - 1)) << 3), narrow)

    def at_y(step):
        return (wide_no_y + ((y + step) & (NY - 1)), narrow)

    def at_line(step):
        other = (line + step) & (LINE - 1)
        return (wide_no_z + (((other >> 1) & 1) << 5), ((other >> 2) << 1) | (other & 1))

    barrier = pltpu.get_barrier_semaphore()

    def greet(partner):
        pl.semaphore_signal(barrier, inc=1, device_id=partner, device_id_type=MESH)

    def greet_line(step, carry):
        greet(at_line(step))
        return carry

    for step in (1, 3, 2):
        greet(at_x(step))
    for step in (1, 7, 2, 6, 3, 5, 4):
        greet(at_y(step))
    lax.fori_loop(1, LINE, greet_line, 0)

    get_items = pltpu.make_async_copy(items_hbm, items_in, in_sem.at[0])
    get_weight = pltpu.make_async_copy(weight_hbm, weight_in, in_sem.at[1])
    get_users = pltpu.make_async_copy(users_hbm, users_in, in_sem.at[2])
    get_mass = pltpu.make_async_copy(mass_hbm, masses.at[z_lo], in_sem.at[3])
    get_items.start()
    get_weight.start()
    get_users.start()
    get_mass.start()

    get_items.wait()
    get_weight.wait()
    rows[0, x, 0:BLOCK, :] = unit_rows(items_in[...].astype(F32), 1)
    rows[0, x, BLOCK:BLOCK + 16, :] = jnp.broadcast_to(
        weight_in[...].astype(F32), (16, BLOCK)
    ).astype(BF16)

    pl.semaphore_wait(barrier, NX - 1 + NY - 1 + LINE - 1)

    def remote(src, dst, send, recv, partner):
        return pltpu.make_async_remote_copy(
            src_ref=src, dst_ref=dst, send_sem=send, recv_sem=recv,
            device_id=partner, device_id_type=MESH,
        )

    def settle(part, sem):
        pltpu.make_async_copy(part, part, sem).wait()

    for step in (1, 3, 2):
        remote(rows.at[0, x], rows.at[0, x], x_send.at[0], x_recv.at[0], at_x(step)).start()

    up, down = at_line(2), at_line(LINE - 2)
    get_users.wait()
    get_mass.wait()
    for half, partner in ((0, up), (1, down)):
        values = users_in[half * TILE:(half + 1) * TILE, :].astype(F32).T
        tile = z_lo * 2 + half
        users[tile, 0:WIDTH, :] = unit_rows(values, 0)
        part = users.at[tile, 0:WIDTH, :]
        remote(part, part, u_send.at[half], u_recv.at[half], partner).start()
    remote(masses.at[z_lo], masses.at[z_lo], u_send.at[2], u_recv.at[2], up).start()

    settle(rows.at[0, 0:3], x_recv.at[0])

    def slot_of(way, hop):
        return 7 if hop == 4 else max(2 * hop - 1 + way, 0) if hop else 0

    def y_copy(way, hop, half):
        pair = slice(2 * half, 2 * half + 2)
        return remote(
            rows.at[slot_of(way, hop - 1), pair], rows.at[slot_of(way, hop), pair],
            y_send.at[0], y_recv.at[way, hop, half], at_y(NY - 1 if way else 1),
        )

    for half in (0, 1):
        for way in (0, 1):
            y_copy(way, 1, half).start()

    ones = jnp.ones((WIDTH, TILE), BF16)
    for tile in range(TILES):
        users[tile, WIDTH:2 * WIDTH, :] = ones
    row_acc[...] = jnp.zeros_like(row_acc)

    sub = lax.broadcasted_iota(jnp.int32, (8, BLOCK), 0)

    def turn(slot):
        value = jnp.ones((8, BLOCK), F32)
        for block in range(NX):
            weight = rows[slot, block, BLOCK:BLOCK + 16, :].astype(F32)[0:8]
            value = jnp.where((sub & 3) == block, weight, value)
        high, middle, low = three_pieces(value)
        first = jnp.where(sub < 4, high, middle)
        second = jnp.where(sub < 4, low, 0.0)
        stacked = jnp.concatenate([first, second, jnp.zeros((BLOCK - 16, BLOCK), F32)], axis=0)
        turned[slot] = stacked.T.astype(BF16)

    lane = lax.broadcasted_iota(jnp.int32, (1, BLOCK), 1)

    def before(hop):
        if hop == 0:
            turn(0)
            return
        for half in (0, 1):
            for way in (0, 1):
                if hop < 4 or half == way:
                    y_copy(way, hop, half).wait_recv()
                if hop < 3 or (hop == 3 and half == way):
                    y_copy(way, hop + 1, half).start()
        for slot in sorted({slot_of(0, hop), slot_of(1, hop)}):
            turn(slot)

    def compute_step(at, carry):
        slot, later = at >> 1, at & 1
        for known, hop in ((0, 0), (2, 1), (6, 2), (10, 3), (14, 4)):
            @pl.when(at == known)
            def _():
                before(hop)

        @pl.when(at == 1)
        def _():
            for half in (0, 1):
                settle(users.at[half, 0:WIDTH, :], u_recv.at[half])
            settle(masses.at[0], u_recv.at[2])

        block_of_users = (z_lo + later) & 1
        accs = [jnp.zeros((8, TILE), F32) for _ in range(2)]
        bias = turned[slot]
        for block in range(NX):
            kept = ((lane & 3) == block).astype(F32).astype(BF16)
            left = jnp.concatenate([rows[slot, block, 0:BLOCK, :], bias * kept], axis=1)
            for part in range(2):
                tile = block_of_users * 2 + part
                scores = jnp.dot(left, users[tile], preferred_element_type=F32)
                values = jnp.exp2((scores * SCALE).astype(BF16))
                kernel[slot, tile, block * BLOCK:(block + 1) * BLOCK] = values
                accs[part] += jnp.sum(values.astype(F32).reshape(BLOCK // 8, 8, TILE), axis=0)
        for part in range(2):
            row_acc[block_of_users * 2 + part] += accs[part]
        return carry

    lax.fori_loop(0, 16, compute_step, 0)

    for tile in range(TILES):
        total = jnp.sum(row_acc[tile], axis=0, keepdims=True)
        for part in range(PARTS):
            at = tile * PARTS + part
            row_parts[line, at:at + 1, :] = total[:, part * 128:(part + 1) * 128]

    def send_rows(step, carry):
        remote(row_parts.at[line], row_parts.at[line], r_send.at[0], r_recv.at[0],
               at_line(step)).start()
        return carry

    lax.fori_loop(1, LINE, send_rows, 0)
    settle(row_parts.at[0:LINE - 1], r_recv.at[0])
    total = row_parts[0]
    for part in range(1, LINE):
        total = total + row_parts[part]
    scale = masses[...].reshape(16, 128) / (total / item_count)
    for at in range(TILES * PARTS):
        user_rows[at] = jnp.broadcast_to(scale[at:at + 1, :], (8, 128))
    column_half[...] = total.reshape(2, 8, 128)
    row_total_ref[...] = column_half[z_lo]

    def sum_columns(slot):
        for block in range(NX):
            pieces = []
            for half in (0, 1):
                acc = jnp.zeros((HALF // 8, 8, 128), F32)
                for tile in range(TILES):
                    for part in range(PARTS):
                        piece = kernel[slot, tile,
                                       block * BLOCK + half * HALF:block * BLOCK + (half + 1) * HALF,
                                       part * 128:(part + 1) * 128]
                        piece = piece.astype(F32).reshape(HALF // 8, 8, 128)
                        acc = acc + piece * user_rows[tile * PARTS + part]
                pieces.append(acc.reshape(HALF, 128))
            flat = jnp.concatenate(pieces, axis=0).T
            column_send[slot, block] = jnp.sum(flat, axis=0, keepdims=True)

    def column_step(step, carry):
        slot = step & (NY - 1)
        sum_columns(slot)
        hop = (step + 1) >> 1
        ahead = jnp.where((step & 1) == 0, hop, NY - hop)

        @pl.when(step < NY)
        def _():
            remote(column_send.at[slot], column_y.at[slot], cy_send.at[0], cy_recv.at[0],
                   at_y(ahead)).start()

        return carry

    lax.fori_loop(1, NY + 1, column_step, 0)
    column_y[0] = column_send[0]
    settle(column_y.at[1:NY], cy_recv.at[0])
    total = column_y[0]
    for part in range(1, NY):
        total = total + column_y[part]
    column_x[NX] = total

    for step in (1, 3, 2):
        remote(column_x.at[NX, (x + step) & (NX - 1)], column_x.at[step, 0],
               cx_send.at[0], cx_recv.at[0], at_x(step)).start()
    column_x[0, 0] = column_x[NX, x]
    settle(column_x.at[1:NX, 0], cx_recv.at[0])
    total = column_x[0, 0]
    for part in range(1, NX):
        total = total + column_x[part, 0]
    weight = weight_in[...].astype(F32)
    column_total_ref[...] = total / weight

    settle(rows.at[0, 0:3], x_send.at[0])
    settle(rows.at[0:7], y_send.at[0])
    for half in (0, 1):
        settle(users.at[half, 0:WIDTH, :], u_send.at[half])
    settle(masses.at[0], u_send.at[2])
    settle(row_parts.at[0:LINE - 1], r_send.at[0])
    settle(column_y.at[1:NY], cy_send.at[0])
    settle(column_x.at[1:NX, 0], cx_send.at[0])


def on_device(users, items, item_scale, user_mass, item_mass):
    user_count = users.shape[0] * lax.axis_size("wide")
    item_count = items.shape[0] * lax.axis_size("wide") * lax.axis_size("narrow")
    dma = pltpu.SemaphoreType.DMA
    vmem = pl.BlockSpec(memory_space=pltpu.VMEM)
    row_total, column_total = pl.pallas_call(
        functools.partial(body, item_count),
        out_shape=(
            jax.ShapeDtypeStruct((8, 128), F32),
            jax.ShapeDtypeStruct((1, 128), F32),
        ),
        in_specs=[pl.BlockSpec(memory_space=pl.ANY)] * 4,
        out_specs=(vmem, vmem),
        scratch_shapes=[
            pltpu.VMEM((USERS, WIDTH), BF16),
            pltpu.VMEM((BLOCK, WIDTH), BF16),
            pltpu.VMEM((1, BLOCK), BF16),
            pltpu.VMEM((NY, NX, BLOCK + 16, WIDTH), BF16),
            pltpu.VMEM((NY, BLOCK, BLOCK), BF16),
            pltpu.VMEM((TILES, 2 * WIDTH, TILE), BF16),
            pltpu.VMEM((NY, TILES, NX * BLOCK, TILE), BF16),
            pltpu.VMEM((TILES, 8, TILE), F32),
            pltpu.VMEM((LINE, 16, 128), F32),
            pltpu.VMEM((2, 8, 128), F32),
            pltpu.VMEM((TILES * PARTS, 8, 128), F32),
            pltpu.VMEM((NY, NX, 1, BLOCK), F32),
            pltpu.VMEM((NY, NX, 1, BLOCK), F32),
            pltpu.VMEM((NX + 1, NX, 1, BLOCK), F32),
            pltpu.VMEM((2, 8, 128), F32),
            dma((4,)),
            dma((1,)), dma((1,)),
            dma((1,)), dma((2, 5, 2)),
            dma((3,)), dma((3,)),
            dma((1,)), dma((1,)),
            dma((1,)), dma((1,)),
            dma((1,)), dma((1,)),
        ],
        compiler_params=pltpu.CompilerParams(
            collective_id=0, has_side_effects=True, vmem_limit_bytes=56 * 1024 * 1024
        ),
        cost_estimate=pl.CostEstimate(
            flops=2 * 4096 * 2048 * 256, bytes_accessed=1 << 20, transcendentals=4096 * 2048
        ),
        name="scaling",
    )(users, items, item_scale.reshape(1, 128), user_mass.reshape(8, 128))
    user_scale = user_mass / (row_total.reshape(1024) / item_count)
    item_scale_new = item_mass / (column_total.reshape(128) / user_count)
    return user_scale, item_scale_new


def solution(mesh):
    in_specs = (
        P("wide", None),
        P(("wide", "narrow"), None),
        P(("wide", "narrow")),
        P("wide"),
        P(("wide", "narrow")),
    )
    out_specs = (P("wide"), P(("wide", "narrow")))
    return jax.shard_map(
        on_device, mesh=mesh, in_specs=in_specs, out_specs=out_specs, check_vma=False
    )
```

time: 720 us -> 56.1 us (0.08)
  the two profiles are of different devices: /device:TPU:64 before, /device:TPU:1 now
where the time goes in v2:
time: 56.1 us; the launch traced here: 55.4 us
  Pallas kernels  52.9 us (94%)
  other arithmetic  1.8 us (3%)
  between operations  0.67 us (1%)
    pallas_call x1, Pallas kernels, on_device(): pl.pallas_call(functools.partial(body, item_count), out_shape=(jax.ShapeD...  52.9 us
    div x1, other arithmetic, on_device(): user_scale = user_mass / (row_total.reshape(1024) / item_count)  1.28 us

profile of v2, /device:TPU:1, one launch (start us, length us, event | category | flops | bytes accessed | tf_op | source)
XLA Modules:
  0.0 55.4 jit_solution(8232702395326911244)
XLA Ops:
  0.6 0.0 copy-start
  0.6 52.9 %scaling.1 = (f32[8,128]{1,0:T(8,128)}, f32[1,128]{1,0:T(1,128)}) custom-call(bf16[1024,128]{1,0:T(8,128)(2,1)} %users_hbm.1, bf16[128,128]{1,0:T(8,128)(2,1)} %items_hbm.1, bf16[1,128]{1,0:T(2,128)(2,1)} %bitcast.7, f32[8,128]{1,0:T(8,128)} %bitcast.6), custom_call_target="tpu_custom_call" | custom-call | flops 4294967296 | bytes 1048576 | tf_op jit(solution)/shard_map/scaling/pallas_call | solution.py:289
  53.5 0.0 copy-done
  53.5 0.0 copy-start.1
  53.6 0.0 copy-start.2
  53.6 1.3 %bitcast_divide_fusion = f32[1024]{0:T(1024)} fusion(f32[1024]{0:T(1024)S(1)} %copy-done, f32[8,128]{1,0:T(8,128)} %get-tuple-element.4), kind=kLoop, calls=%fused_computation | loop fusion | flops 2048 | bytes 12288 | tf_op jit(solution)/shard_map/div | solution.py:329
  54.8 0.0 copy-done.1
  54.8 0.0 copy-done.2
  54.9 0.5 bitcast_divide_fusion.1
Async XLA Ops:
  0.6 52.9 %copy-start = (f32[1024]{0:T(1024)S(1)}, f32[1024]{0:T(1024)}, u32[]{:S(2)}) copy-start(f32[1024]{0:T(1024)} %param.8) | copy-start | bytes 12292
  53.5 1.3 %copy-start.1 = (f32[128]{0:T(128)S(1)}, f32[128]{0:T(128)}, u32[]{:S(2)}) copy-start(f32[128]{0:T(128)} %param.9) | copy-start | bytes 1540
  53.6 1.3 %copy-start.2 = (f32[1,128]{1,0:T(1,128)S(1)}, f32[1,128]{1,0:T(1,128)}, u32[]{:S(2)}) copy-start(f32[1,128]{1,0:T(1,128)} %get-tuple-element.5) | copy-start | bytes 1540

commit v3 on v2

--- a/solution.py
+++ b/solution.py
@@ -15,7 +15,6 @@
 NX, NY, NZ = 4, 8, 8
 LINE = 2 * NZ
 BLOCK = 128
-HALF = 64
 USERS = 1024
 TILE = 512
 TILES = 2 * USERS // TILE
@@ -29,18 +28,16 @@
     return (values * lax.rsqrt(squares)).astype(BF16)
 
 
-def three_pieces(weight):
-    value = 0.5 * jnp.log(weight)
-    high = value.astype(BF16).astype(F32)
-    middle = (value - high).astype(BF16).astype(F32)
-    return high, middle, value - high - middle
+def two_pieces(value):
+    high = value.astype(BF16)
+    return high, (value - high.astype(F32)).astype(BF16)
 
 
 def body(
     item_count,
     users_hbm, items_hbm, weight_hbm, mass_hbm,
     row_total_ref, column_total_ref,
-    users_in, items_in, weight_in, rows, turned, users, kernel, row_acc, row_parts, masses,
+    users_in, items_in, weight_in, rows, hats, users, kernel, row_acc, row_parts, masses,
     user_rows, column_send, column_y, column_x, column_half,
     in_sem, x_send, x_recv, y_send, y_recv, u_send, u_recv, r_send, r_recv,
     cy_send, cy_recv, cx_send, cx_recv,
@@ -115,9 +112,8 @@
     get_mass.wait()
     for half, partner in ((0, up), (1, down)):
         values = users_in[half * TILE:(half + 1) * TILE, :].astype(F32).T
-        tile = z_lo * 2 + half
-        users[tile, 0:WIDTH, :] = unit_rows(values, 0)
-        part = users.at[tile, 0:WIDTH, :]
+        hats[z_lo * 2 + half] = unit_rows(values, 0)
+        part = hats.at[z_lo * 2 + half]
         remote(part, part, u_send.at[half], u_recv.at[half], partner).start()
     remote(masses.at[z_lo], masses.at[z_lo], u_send.at[2], u_recv.at[2], up).start()
 
@@ -137,42 +133,27 @@
         for way in (0, 1):
             y_copy(way, 1, half).start()
 
-    ones = jnp.ones((WIDTH, TILE), BF16)
-    for tile in range(TILES):
-        users[tile, WIDTH:2 * WIDTH, :] = ones
     row_acc[...] = jnp.zeros_like(row_acc)
 
-    sub = lax.broadcasted_iota(jnp.int32, (8, BLOCK), 0)
-
-    def turn(slot):
-        value = jnp.ones((8, BLOCK), F32)
-        for block in range(NX):
-            weight = rows[slot, block, BLOCK:BLOCK + 16, :].astype(F32)[0:8]
-            value = jnp.where((sub & 3) == block, weight, value)
-        high, middle, low = three_pieces(value)
-        first = jnp.where(sub < 4, high, middle)
-        second = jnp.where(sub < 4, low, 0.0)
-        stacked = jnp.concatenate([first, second, jnp.zeros((BLOCK - 16, BLOCK), F32)], axis=0)
-        turned[slot] = stacked.T.astype(BF16)
-
-    lane = lax.broadcasted_iota(jnp.int32, (1, BLOCK), 1)
+    def scale_users(block):
+        for half in (0, 1):
+            high, low = two_pieces(hats[block * 2 + half].astype(F32) * SCALE)
+            users[block * 2 + half, 0:WIDTH, :] = high
+            users[block * 2 + half, WIDTH:2 * WIDTH, :] = low
+
+    scale_users(z_lo)
 
     def before(hop):
-        if hop == 0:
-            turn(0)
-            return
         for half in (0, 1):
             for way in (0, 1):
                 if hop < 4 or half == way:
                     y_copy(way, hop, half).wait_recv()
                 if hop < 3 or (hop == 3 and half == way):
                     y_copy(way, hop + 1, half).start()
-        for slot in sorted({slot_of(0, hop), slot_of(1, hop)}):
-            turn(slot)
 
     def compute_step(at, carry):
         slot, later = at >> 1, at & 1
-        for known, hop in ((0, 0), (2, 1), (6, 2), (10, 3), (14, 4)):
+        for known, hop in ((2, 1), (6, 2), (10, 3), (14, 4)):
             @pl.when(at == known)
             def _():
                 before(hop)
@@ -180,29 +161,33 @@
         @pl.when(at == 1)
         def _():
             for half in (0, 1):
-                settle(users.at[half, 0:WIDTH, :], u_recv.at[half])
+                settle(hats.at[half], u_recv.at[half])
             settle(masses.at[0], u_recv.at[2])
+            scale_users(1 - z_lo)
 
         block_of_users = (z_lo + later) & 1
-        accs = [jnp.zeros((8, TILE), F32) for _ in range(2)]
-        bias = turned[slot]
-        for block in range(NX):
-            kept = ((lane & 3) == block).astype(F32).astype(BF16)
-            left = jnp.concatenate([rows[slot, block, 0:BLOCK, :], bias * kept], axis=1)
+        accs = [jnp.zeros((16, TILE), F32) for _ in range(2)]
+        for pair in range(NX // 2):
+            both = (2 * pair, 2 * pair + 1)
+            hat = jnp.concatenate([rows[slot, block, 0:BLOCK, :] for block in both], axis=0)
+            left = jnp.concatenate([hat, hat], axis=1)
+            weight = jnp.concatenate(
+                [rows[slot, block, BLOCK:BLOCK + 16, :] for block in both], axis=1
+            )
             for part in range(2):
                 tile = block_of_users * 2 + part
                 scores = jnp.dot(left, users[tile], preferred_element_type=F32)
-                values = jnp.exp2((scores * SCALE).astype(BF16))
-                kernel[slot, tile, block * BLOCK:(block + 1) * BLOCK] = values
-                accs[part] += jnp.sum(values.astype(F32).reshape(BLOCK // 8, 8, TILE), axis=0)
+                values = jnp.exp2(scores.astype(BF16))
+                kernel[slot, tile, pair * 2 * BLOCK:(pair + 1) * 2 * BLOCK] = values
+                accs[part] += jnp.dot(weight, values, preferred_element_type=F32)
         for part in range(2):
-            row_acc[block_of_users * 2 + part] += accs[part]
+            row_acc[block_of_users * 2 + part] += accs[part][0:8]
         return carry
 
     lax.fori_loop(0, 16, compute_step, 0)
 
     for tile in range(TILES):
-        total = jnp.sum(row_acc[tile], axis=0, keepdims=True)
+        total = row_acc[tile][0:1, :]
         for part in range(PARTS):
             at = tile * PARTS + part
             row_parts[line, at:at + 1, :] = total[:, part * 128:(part + 1) * 128]
@@ -218,26 +203,27 @@
     for part in range(1, LINE):
         total = total + row_parts[part]
     scale = masses[...].reshape(16, 128) / (total / item_count)
+    sub = lax.broadcasted_iota(jnp.int32, (16, 128), 0)
+    high, low = two_pieces(scale)
+    high, low = high.astype(F32), low.astype(F32)
     for at in range(TILES * PARTS):
-        user_rows[at] = jnp.broadcast_to(scale[at:at + 1, :], (8, 128))
+        first = jnp.broadcast_to(high[at:at + 1, :], (16, 128))
+        second = jnp.broadcast_to(low[at:at + 1, :], (16, 128))
+        pieces = jnp.where(sub == 0, first, jnp.where(sub == 1, second, 0.0)).astype(BF16)
+        user_rows[:, at * 128:(at + 1) * 128] = pieces
     column_half[...] = total.reshape(2, 8, 128)
     row_total_ref[...] = column_half[z_lo]
 
     def sum_columns(slot):
+        sums = jnp.zeros((16, NX * BLOCK), F32)
+        for tile in range(TILES):
+            sums += lax.dot_general(
+                user_rows[:, tile * TILE:(tile + 1) * TILE], kernel[slot, tile],
+                (((1,), (1,)), ((), ())), preferred_element_type=F32,
+            )
+        flat = sums[0:1, :] + sums[1:2, :]
         for block in range(NX):
-            pieces = []
-            for half in (0, 1):
-                acc = jnp.zeros((HALF // 8, 8, 128), F32)
-                for tile in range(TILES):
-                    for part in range(PARTS):
-                        piece = kernel[slot, tile,
-                                       block * BLOCK + half * HALF:block * BLOCK + (half + 1) * HALF,
-                                       part * 128:(part + 1) * 128]
-                        piece = piece.astype(F32).reshape(HALF // 8, 8, 128)
-                        acc = acc + piece * user_rows[tile * PARTS + part]
-                pieces.append(acc.reshape(HALF, 128))
-            flat = jnp.concatenate(pieces, axis=0).T
-            column_send[slot, block] = jnp.sum(flat, axis=0, keepdims=True)
+            column_send[slot, block] = flat[:, block * BLOCK:(block + 1) * BLOCK]
 
     def column_step(step, carry):
         slot = step & (NY - 1)
@@ -268,13 +254,12 @@
     total = column_x[0, 0]
     for part in range(1, NX):
         total = total + column_x[part, 0]
-    weight = weight_in[...].astype(F32)
-    column_total_ref[...] = total / weight
+    column_total_ref[...] = total
 
     settle(rows.at[0, 0:3], x_send.at[0])
     settle(rows.at[0:7], y_send.at[0])
     for half in (0, 1):
-        settle(users.at[half, 0:WIDTH, :], u_send.at[half])
+        settle(hats.at[half], u_send.at[half])
     settle(masses.at[0], u_send.at[2])
     settle(row_parts.at[0:LINE - 1], r_send.at[0])
     settle(column_y.at[1:NY], cy_send.at[0])
@@ -299,13 +284,13 @@
             pltpu.VMEM((BLOCK, WIDTH), BF16),
             pltpu.VMEM((1, BLOCK), BF16),
             pltpu.VMEM((NY, NX, BLOCK + 16, WIDTH), BF16),
-            pltpu.VMEM((NY, BLOCK, BLOCK), BF16),
+            pltpu.VMEM((TILES, WIDTH, TILE), BF16),
             pltpu.VMEM((TILES, 2 * WIDTH, TILE), BF16),
             pltpu.VMEM((NY, TILES, NX * BLOCK, TILE), BF16),
             pltpu.VMEM((TILES, 8, TILE), F32),
             pltpu.VMEM((LINE, 16, 128), F32),
             pltpu.VMEM((2, 8, 128), F32),
-            pltpu.VMEM((TILES * PARTS, 8, 128), F32),
+            pltpu.VMEM((16, 2 * USERS), BF16),
             pltpu.VMEM((NY, NX, 1, BLOCK), F32),
             pltpu.VMEM((NY, NX, 1, BLOCK), F32),
             pltpu.VMEM((NX + 1, NX, 1, BLOCK), F32),

time: 56.1 us -> 58.8 us (1.048)
  Pallas kernels: 52.9 us -> 55.5 us
    pallas_call x1, Pallas kernels: 52.9 us -> 55.5 us  [on_device(): pl.pallas_call(functools.partial(body, item_count), out_shape=(jax.ShapeD...]
where the time goes in v3:
time: 58.8 us; the launch traced here: 58 us
  Pallas kernels  55.5 us (94%)
  other arithmetic  1.8 us (3%)
  between operations  0.67 us (1%)
    pallas_call x1, Pallas kernels, on_device(): pl.pallas_call(functools.partial(body, item_count), out_shape=(jax.ShapeD...  55.5 us
    div x1, other arithmetic, on_device(): user_scale = user_mass / (row_total.reshape(1024) / item_count)  1.28 us

profile of v3, /device:TPU:1, one launch (start us, length us, event | category | flops | bytes accessed | tf_op | source)
XLA Modules:
  0.0 58.0 jit_solution(487529011928215093)
XLA Ops:
  0.6 0.0 copy-start
  0.6 55.5 %scaling.1 = (f32[8,128]{1,0:T(8,128)}, f32[1,128]{1,0:T(1,128)}) custom-call(bf16[1024,128]{1,0:T(8,128)(2,1)} %users_hbm.1, bf16[128,128]{1,0:T(8,128)(2,1)} %items_hbm.1, bf16[1,128]{1,0:T(2,128)(2,1)} %bitcast.7, f32[8,128]{1,0:T(8,128)} %bitcast.6), custom_call_target="tpu_custom_call" | custom-call | flops 4294967296 | bytes 1048576 | tf_op jit(solution)/shard_map/scaling/pallas_call | solution.py:274
  56.2 0.0 copy-done
  56.2 0.0 copy-start.1
  56.2 0.0 copy-start.2
  56.2 1.3 %bitcast_divide_fusion = f32[1024]{0:T(1024)} fusion(f32[1024]{0:T(1024)S(1)} %copy-done, f32[8,128]{1,0:T(8,128)} %get-tuple-element.4), kind=kLoop, calls=%fused_computation | loop fusion | flops 2048 | bytes 12288 | tf_op jit(solution)/shard_map/div | solution.py:314
  57.5 0.0 copy-done.1
  57.5 0.0 copy-done.2
  57.5 0.5 bitcast_divide_fusion.1
Async XLA Ops:
  0.6 55.5 %copy-start = (f32[1024]{0:T(1024)S(1)}, f32[1024]{0:T(1024)}, u32[]{:S(2)}) copy-start(f32[1024]{0:T(1024)} %param.8) | copy-start | bytes 12292
  56.2 1.3 %copy-start.1 = (f32[128]{0:T(128)S(1)}, f32[128]{0:T(128)}, u32[]{:S(2)}) copy-start(f32[128]{0:T(128)} %param.9) | copy-start | bytes 1540
  56.2 1.3 %copy-start.2 = (f32[1,128]{1,0:T(1,128)S(1)}, f32[1,128]{1,0:T(1,128)}, u32[]{:S(2)}) copy-start(f32[1,128]{1,0:T(1,128)} %get-tuple-element.5) | copy-start | bytes 1540

commit v4 on v2

--- a/solution.py
+++ b/solution.py
@@ -153,29 +153,28 @@
         first = jnp.where(sub < 4, high, middle)
         second = jnp.where(sub < 4, low, 0.0)
         stacked = jnp.concatenate([first, second, jnp.zeros((BLOCK - 16, BLOCK), F32)], axis=0)
-        turned[slot] = stacked.T.astype(BF16)
+        turned[...] = stacked.T.astype(BF16)
 
     lane = lax.broadcasted_iota(jnp.int32, (1, BLOCK), 1)
 
-    def before(hop):
-        if hop == 0:
-            turn(0)
-            return
-        for half in (0, 1):
-            for way in (0, 1):
-                if hop < 4 or half == way:
-                    y_copy(way, hop, half).wait_recv()
-                if hop < 3 or (hop == 3 and half == way):
-                    y_copy(way, hop + 1, half).start()
-        for slot in sorted({slot_of(0, hop), slot_of(1, hop)}):
-            turn(slot)
+    pieces = [(hop, way, half) for hop in (1, 2, 3) for way in (0, 1) for half in (0, 1)]
+    pieces += [(4, 0, 0), (4, 1, 1)]
+
+    def pass_on(hop, way, half):
+        y_copy(way, hop, half).wait_recv()
+        if hop < 3 or (hop == 3 and half == way):
+            y_copy(way, hop + 1, half).start()
 
     def compute_step(at, carry):
         slot, later = at >> 1, at & 1
-        for known, hop in ((0, 0), (2, 1), (6, 2), (10, 3), (14, 4)):
+        for known, piece in enumerate(pieces):
             @pl.when(at == known)
             def _():
-                before(hop)
+                pass_on(*piece)
+
+        @pl.when(later == 0)
+        def _():
+            turn(slot)
 
         @pl.when(at == 1)
         def _():
@@ -185,7 +184,7 @@
 
         block_of_users = (z_lo + later) & 1
         accs = [jnp.zeros((8, TILE), F32) for _ in range(2)]
-        bias = turned[slot]
+        bias = turned[...]
         for block in range(NX):
             kept = ((lane & 3) == block).astype(F32).astype(BF16)
             left = jnp.concatenate([rows[slot, block, 0:BLOCK, :], bias * kept], axis=1)
@@ -299,7 +298,7 @@
             pltpu.VMEM((BLOCK, WIDTH), BF16),
             pltpu.VMEM((1, BLOCK), BF16),
             pltpu.VMEM((NY, NX, BLOCK + 16, WIDTH), BF16),
-            pltpu.VMEM((NY, BLOCK, BLOCK), BF16),
+            pltpu.VMEM((BLOCK, BLOCK), BF16),
             pltpu.VMEM((TILES, 2 * WIDTH, TILE), BF16),
             pltpu.VMEM((NY, TILES, NX * BLOCK, TILE), BF16),
             pltpu.VMEM((TILES, 8, TILE), F32),

time: 56.1 us -> 58.6 us (1.045)
  Pallas kernels: 52.9 us -> 55.7 us
    pallas_call x1, Pallas kernels: 52.9 us -> 55.7 us  [on_device(): pl.pallas_call(functools.partial(body, item_count), out_shape=(jax.ShapeD...]
where the time goes in v4:
time: 58.6 us; the launch traced here: 58.2 us
  Pallas kernels  55.7 us (95%)
  other arithmetic  1.8 us (3%)
  between operations  0.67 us (1%)
    pallas_call x1, Pallas kernels, on_device(): pl.pallas_call(functools.partial(body, item_count), out_shape=(jax.ShapeD...  55.7 us
    div x1, other arithmetic, on_device(): user_scale = user_mass / (row_total.reshape(1024) / item_count)  1.28 us

profile of v4, /device:TPU:1, one launch (start us, length us, event | category | flops | bytes accessed | tf_op | source)
XLA Modules:
  0.0 58.2 jit_solution(6623280826757671893)
XLA Ops:
  0.6 0.0 copy-start
  0.6 55.7 %scaling.1 = (f32[8,128]{1,0:T(8,128)}, f32[1,128]{1,0:T(1,128)}) custom-call(bf16[1024,128]{1,0:T(8,128)(2,1)} %users_hbm.1, bf16[128,128]{1,0:T(8,128)(2,1)} %items_hbm.1, bf16[1,128]{1,0:T(2,128)(2,1)} %bitcast.7, f32[8,128]{1,0:T(8,128)} %bitcast.6), custom_call_target="tpu_custom_call" | custom-call | flops 4294967296 | bytes 1048576 | tf_op jit(solution)/shard_map/scaling/pallas_call | solution.py:288
  56.3 0.0 copy-done
  56.3 0.0 copy-start.1
  56.4 0.0 copy-start.2
  56.4 1.3 %bitcast_divide_fusion = f32[1024]{0:T(1024)} fusion(f32[1024]{0:T(1024)S(1)} %copy-done, f32[8,128]{1,0:T(8,128)} %get-tuple-element.4), kind=kLoop, calls=%fused_computation | loop fusion | flops 2048 | bytes 12288 | tf_op jit(solution)/shard_map/div | solution.py:328
  57.6 0.0 copy-done.1
  57.6 0.0 copy-done.2
  57.6 0.5 bitcast_divide_fusion.1
Async XLA Ops:
  0.6 55.7 %copy-start = (f32[1024]{0:T(1024)S(1)}, f32[1024]{0:T(1024)}, u32[]{:S(2)}) copy-start(f32[1024]{0:T(1024)} %param.8) | copy-start | bytes 12292
  56.3 1.3 %copy-start.1 = (f32[128]{0:T(128)S(1)}, f32[128]{0:T(128)}, u32[]{:S(2)}) copy-start(f32[128]{0:T(128)} %param.9) | copy-start | bytes 1540
  56.4 1.3 %copy-start.2 = (f32[1,128]{1,0:T(1,128)S(1)}, f32[1,128]{1,0:T(1,128)}, u32[]{:S(2)}) copy-start(f32[1,128]{1,0:T(1,128)} %get-tuple-element.5) | copy-start | bytes 1540

commit v5 on v2

--- a/solution.py
+++ b/solution.py
@@ -29,18 +29,11 @@
     return (values * lax.rsqrt(squares)).astype(BF16)
 
 
-def three_pieces(weight):
-    value = 0.5 * jnp.log(weight)
-    high = value.astype(BF16).astype(F32)
-    middle = (value - high).astype(BF16).astype(F32)
-    return high, middle, value - high - middle
-
-
 def body(
     item_count,
     users_hbm, items_hbm, weight_hbm, mass_hbm,
     row_total_ref, column_total_ref,
-    users_in, items_in, weight_in, rows, turned, users, kernel, row_acc, row_parts, masses,
+    users_in, items_in, weight_in, rows, spread, users, kernel, row_acc, row_parts, masses,
     user_rows, column_send, column_y, column_x, column_half,
     in_sem, x_send, x_recv, y_send, y_recv, u_send, u_recv, r_send, r_recv,
     cy_send, cy_recv, cx_send, cx_recv,
@@ -116,8 +109,8 @@
     for half, partner in ((0, up), (1, down)):
         values = users_in[half * TILE:(half + 1) * TILE, :].astype(F32).T
         tile = z_lo * 2 + half
-        users[tile, 0:WIDTH, :] = unit_rows(values, 0)
-        part = users.at[tile, 0:WIDTH, :]
+        users[tile] = unit_rows(values, 0)
+        part = users.at[tile]
         remote(part, part, u_send.at[half], u_recv.at[half], partner).start()
     remote(masses.at[z_lo], masses.at[z_lo], u_send.at[2], u_recv.at[2], up).start()
 
@@ -137,29 +130,18 @@
         for way in (0, 1):
             y_copy(way, 1, half).start()
 
-    ones = jnp.ones((WIDTH, TILE), BF16)
-    for tile in range(TILES):
-        users[tile, WIDTH:2 * WIDTH, :] = ones
     row_acc[...] = jnp.zeros_like(row_acc)
 
-    sub = lax.broadcasted_iota(jnp.int32, (8, BLOCK), 0)
-
-    def turn(slot):
-        value = jnp.ones((8, BLOCK), F32)
+    def spread_weights(slot):
         for block in range(NX):
-            weight = rows[slot, block, BLOCK:BLOCK + 16, :].astype(F32)[0:8]
-            value = jnp.where((sub & 3) == block, weight, value)
-        high, middle, low = three_pieces(value)
-        first = jnp.where(sub < 4, high, middle)
-        second = jnp.where(sub < 4, low, 0.0)
-        stacked = jnp.concatenate([first, second, jnp.zeros((BLOCK - 16, BLOCK), F32)], axis=0)
-        turned[slot] = stacked.T.astype(BF16)
-
-    lane = lax.broadcasted_iota(jnp.int32, (1, BLOCK), 1)
+            weight = rows[slot, block, BLOCK:BLOCK + 16, :].astype(F32)[0:1]
+            spread[slot, block * BLOCK:(block + 1) * BLOCK] = jnp.broadcast_to(
+                weight, (BLOCK, BLOCK)
+            ).T
 
     def before(hop):
         if hop == 0:
-            turn(0)
+            spread_weights(0)
             return
         for half in (0, 1):
             for way in (0, 1):
@@ -168,7 +150,7 @@
                 if hop < 3 or (hop == 3 and half == way):
                     y_copy(way, hop + 1, half).start()
         for slot in sorted({slot_of(0, hop), slot_of(1, hop)}):
-            turn(slot)
+            spread_weights(slot)
 
     def compute_step(at, carry):
         slot, later = at >> 1, at & 1
@@ -180,21 +162,24 @@
         @pl.when(at == 1)
         def _():
             for half in (0, 1):
-                settle(users.at[half, 0:WIDTH, :], u_recv.at[half])
+                settle(users.at[half], u_recv.at[half])
             settle(masses.at[0], u_recv.at[2])
 
         block_of_users = (z_lo + later) & 1
         accs = [jnp.zeros((8, TILE), F32) for _ in range(2)]
-        bias = turned[slot]
-        for block in range(NX):
-            kept = ((lane & 3) == block).astype(F32).astype(BF16)
-            left = jnp.concatenate([rows[slot, block, 0:BLOCK, :], bias * kept], axis=1)
+        for pair in range(NX // 2):
+            left = jnp.concatenate(
+                [rows[slot, block, 0:BLOCK, :] for block in (2 * pair, 2 * pair + 1)], axis=0
+            )
+            here = slice(pair * 2 * BLOCK, (pair + 1) * 2 * BLOCK)
+            weight = jnp.concatenate([spread[slot, here]] * PARTS, axis=1)
             for part in range(2):
                 tile = block_of_users * 2 + part
                 scores = jnp.dot(left, users[tile], preferred_element_type=F32)
                 values = jnp.exp2((scores * SCALE).astype(BF16))
-                kernel[slot, tile, block * BLOCK:(block + 1) * BLOCK] = values
-                accs[part] += jnp.sum(values.astype(F32).reshape(BLOCK // 8, 8, TILE), axis=0)
+                kernel[slot, tile, here] = values
+                weighted = values.astype(F32) * weight
+                accs[part] += jnp.sum(weighted.reshape(2 * BLOCK // 8, 8, TILE), axis=0)
         for part in range(2):
             row_acc[block_of_users * 2 + part] += accs[part]
         return carry
@@ -268,13 +253,12 @@
     total = column_x[0, 0]
     for part in range(1, NX):
         total = total + column_x[part, 0]
-    weight = weight_in[...].astype(F32)
-    column_total_ref[...] = total / weight
+    column_total_ref[...] = total
 
     settle(rows.at[0, 0:3], x_send.at[0])
     settle(rows.at[0:7], y_send.at[0])
     for half in (0, 1):
-        settle(users.at[half, 0:WIDTH, :], u_send.at[half])
+        settle(users.at[half], u_send.at[half])
     settle(masses.at[0], u_send.at[2])
     settle(row_parts.at[0:LINE - 1], r_send.at[0])
     settle(column_y.at[1:NY], cy_send.at[0])
@@ -299,8 +283,8 @@
             pltpu.VMEM((BLOCK, WIDTH), BF16),
             pltpu.VMEM((1, BLOCK), BF16),
             pltpu.VMEM((NY, NX, BLOCK + 16, WIDTH), BF16),
-            pltpu.VMEM((NY, BLOCK, BLOCK), BF16),
-            pltpu.VMEM((TILES, 2 * WIDTH, TILE), BF16),
+            pltpu.VMEM((NY, NX * BLOCK, BLOCK), F32),
+            pltpu.VMEM((TILES, WIDTH, TILE), BF16),
             pltpu.VMEM((NY, TILES, NX * BLOCK, TILE), BF16),
             pltpu.VMEM((TILES, 8, TILE), F32),
             pltpu.VMEM((LINE, 16, 128), F32),

time: 56.1 us -> 56.2 us (level)
  no operation moved by 1% of the time
where the time goes in v5:
time: 56.2 us; the launch traced here: 55.5 us
  Pallas kernels  53 us (94%)
  other arithmetic  1.8 us (3%)
  between operations  0.67 us (1%)
    pallas_call x1, Pallas kernels, on_device(): pl.pallas_call(functools.partial(body, item_count), out_shape=(jax.ShapeD...  53 us
    div x1, other arithmetic, on_device(): user_scale = user_mass / (row_total.reshape(1024) / item_count)  1.28 us

profile of v5, /device:TPU:1, one launch (start us, length us, event | category | flops | bytes accessed | tf_op | source)
XLA Modules:
  0.0 55.5 jit_solution(9932699609116039500)
XLA Ops:
  0.6 0.0 copy-start
  0.6 53.0 %scaling.1 = (f32[8,128]{1,0:T(8,128)}, f32[1,128]{1,0:T(1,128)}) custom-call(bf16[1024,128]{1,0:T(8,128)(2,1)} %users_hbm.1, bf16[128,128]{1,0:T(8,128)(2,1)} %items_hbm.1, bf16[1,128]{1,0:T(2,128)(2,1)} %bitcast.7, f32[8,128]{1,0:T(8,128)} %bitcast.6), custom_call_target="tpu_custom_call" | custom-call | flops 4294967296 | bytes 1048576 | tf_op jit(solution)/shard_map/scaling/pallas_call | solution.py:273
  53.6 0.0 copy-done
  53.6 0.0 copy-start.1
  53.7 0.0 copy-start.2
  53.7 1.3 %bitcast_divide_fusion = f32[1024]{0:T(1024)} fusion(f32[1024]{0:T(1024)S(1)} %copy-done, f32[8,128]{1,0:T(8,128)} %get-tuple-element.4), kind=kLoop, calls=%fused_computation | loop fusion | flops 2048 | bytes 12288 | tf_op jit(solution)/shard_map/div | solution.py:313
  54.9 0.0 copy-done.1
  54.9 0.0 copy-done.2
  54.9 0.5 bitcast_divide_fusion.1
Async XLA Ops:
  0.6 53.0 %copy-start = (f32[1024]{0:T(1024)S(1)}, f32[1024]{0:T(1024)}, u32[]{:S(2)}) copy-start(f32[1024]{0:T(1024)} %param.8) | copy-start | bytes 12292
  53.6 1.3 %copy-start.1 = (f32[128]{0:T(128)S(1)}, f32[128]{0:T(128)}, u32[]{:S(2)}) copy-start(f32[128]{0:T(128)} %param.9) | copy-start | bytes 1540
  53.7 1.3 %copy-start.2 = (f32[1,128]{1,0:T(1,128)S(1)}, f32[1,128]{1,0:T(1,128)}, u32[]{:S(2)}) copy-start(f32[1,128]{1,0:T(1,128)} %get-tuple-element.5) | copy-start | bytes 1540

commit v6 on v5

--- a/solution.py
+++ b/solution.py
@@ -35,7 +35,7 @@
     row_total_ref, column_total_ref,
     users_in, items_in, weight_in, rows, spread, users, kernel, row_acc, row_parts, masses,
     user_rows, column_send, column_y, column_x, column_half,
-    in_sem, x_send, x_recv, y_send, y_recv, u_send, u_recv, r_send, r_recv,
+    in_sem, x_send, x_recv, y_send, y_recv, f_recv, u_send, u_recv, r_send, r_recv,
     cy_send, cy_recv, cx_send, cx_recv,
 ):
     wide = lax.axis_index("wide")
@@ -84,8 +84,8 @@
 
     get_items.wait()
     get_weight.wait()
-    rows[0, x, 0:BLOCK, :] = unit_rows(items_in[...].astype(F32), 1)
-    rows[0, x, BLOCK:BLOCK + 16, :] = jnp.broadcast_to(
+    rows[0, 0, 0:BLOCK, :] = unit_rows(items_in[...].astype(F32), 1)
+    rows[0, 0, BLOCK:BLOCK + 16, :] = jnp.broadcast_to(
         weight_in[...].astype(F32), (16, BLOCK)
     ).astype(BF16)
 
@@ -100,8 +100,47 @@
     def settle(part, sem):
         pltpu.make_async_copy(part, part, sem).wait()
 
-    for step in (1, 3, 2):
-        remote(rows.at[0, x], rows.at[0, x], x_send.at[0], x_recv.at[0], at_x(step)).start()
+    own = rows.at[0, 0]
+    left, right, far = at_x(3), at_x(1), at_x(2)
+
+    def y_send_to(hop):
+        if hop == 4:
+            remote(own, rows.at[0, 7], y_send.at[0], y_recv.at[4], at_y(4)).start()
+            return
+        remote(own, rows.at[0, 2 * hop - 1], y_send.at[0], y_recv.at[hop], at_y(hop)).start()
+        remote(own, rows.at[0, 2 * hop], y_send.at[0], y_recv.at[hop], at_y(NY - hop)).start()
+
+    def slots_of(hop):
+        return slice(2 * hop - 1, 2 * hop + 1) if 0 < hop < 4 else slice(7, 8) if hop else slice(0, 1)
+
+    def x_send_of(hop):
+        part = rows.at[0, slots_of(hop)]
+        remote(part, rows.at[1, slots_of(hop)], x_send.at[0], x_recv.at[hop], right).start()
+        remote(part, rows.at[2, slots_of(hop)], x_send.at[0], x_recv.at[hop], left).start()
+        if hop in (0, 4):
+            remote(part, rows.at[3, slots_of(hop)], x_send.at[0], x_recv.at[hop], far).start()
+
+    def from_y(hop):
+        settle(rows.at[0, slots_of(hop)], y_recv.at[hop])
+        x_send_of(hop)
+
+    def from_x(hop):
+        if hop in (0, 4):
+            settle(rows.at[1:4, slots_of(hop)], x_recv.at[hop])
+            return
+        settle(rows.at[1:3, slots_of(hop)], x_recv.at[hop])
+        behind, ahead = 2 * hop - 1, 2 * hop
+        remote(rows.at[1, behind], rows.at[3, behind], x_send.at[0], f_recv.at[hop], right).start()
+        remote(rows.at[2, ahead], rows.at[3, ahead], x_send.at[0], f_recv.at[hop], left).start()
+
+    def from_far(hop):
+        settle(rows.at[3, slots_of(hop)], f_recv.at[hop])
+
+    y_send_to(1)
+    x_send_of(0)
+    y_send_to(2)
+    y_send_to(3)
+    y_send_to(4)
 
     up, down = at_line(2), at_line(LINE - 2)
     get_users.wait()
@@ -114,50 +153,49 @@
         remote(part, part, u_send.at[half], u_recv.at[half], partner).start()
     remote(masses.at[z_lo], masses.at[z_lo], u_send.at[2], u_recv.at[2], up).start()
 
-    settle(rows.at[0, 0:3], x_recv.at[0])
-
-    def slot_of(way, hop):
-        return 7 if hop == 4 else max(2 * hop - 1 + way, 0) if hop else 0
-
-    def y_copy(way, hop, half):
-        pair = slice(2 * half, 2 * half + 2)
-        return remote(
-            rows.at[slot_of(way, hop - 1), pair], rows.at[slot_of(way, hop), pair],
-            y_send.at[0], y_recv.at[way, hop, half], at_y(NY - 1 if way else 1),
-        )
-
-    for half in (0, 1):
-        for way in (0, 1):
-            y_copy(way, 1, half).start()
-
+    from_y(1)
+    from_y(2)
     row_acc[...] = jnp.zeros_like(row_acc)
 
-    def spread_weights(slot):
-        for block in range(NX):
-            weight = rows[slot, block, BLOCK:BLOCK + 16, :].astype(F32)[0:1]
-            spread[slot, block * BLOCK:(block + 1) * BLOCK] = jnp.broadcast_to(
-                weight, (BLOCK, BLOCK)
-            ).T
-
-    def before(hop):
-        if hop == 0:
-            spread_weights(0)
-            return
-        for half in (0, 1):
-            for way in (0, 1):
-                if hop < 4 or half == way:
-                    y_copy(way, hop, half).wait_recv()
-                if hop < 3 or (hop == 3 and half == way):
-                    y_copy(way, hop + 1, half).start()
-        for slot in sorted({slot_of(0, hop), slot_of(1, hop)}):
-            spread_weights(slot)
+    def unit_of(unit):
+        late = jnp.logical_or(unit == 3, unit >= 5)
+        column = jnp.where(unit < 3, unit, jnp.where(unit == 3, 0, jnp.where(unit == 4, 3, unit - 4)))
+        return column, jnp.where(late, 4, 0)
+
+    def spread_weights(column, first):
+        for block in range(4):
+            weight = rows[column, first + block, BLOCK:BLOCK + 16, :].astype(F32)[0:1]
+            spread[block * BLOCK:(block + 1) * BLOCK] = jnp.broadcast_to(weight, (BLOCK, BLOCK)).T
+
+    def before(at):
+        if at == 2:
+            from_y(3)
+            from_x(0)
+            from_x(1)
+            from_x(2)
+        elif at == 5:
+            from_y(4)
+        elif at == 6:
+            from_x(3)
+        elif at == 8:
+            from_far(1)
+            from_far(2)
+        elif at == 10:
+            from_x(4)
+        elif at == 14:
+            from_far(3)
 
     def compute_step(at, carry):
-        slot, later = at >> 1, at & 1
-        for known, hop in ((0, 0), (2, 1), (6, 2), (10, 3), (14, 4)):
+        unit, later = at >> 1, at & 1
+        column, first = unit_of(unit)
+        for known in (2, 5, 6, 8, 10, 14):
             @pl.when(at == known)
             def _():
-                before(hop)
+                before(known)
+
+        @pl.when(later == 0)
+        def _():
+            spread_weights(column, first)
 
         @pl.when(at == 1)
         def _():
@@ -167,17 +205,17 @@
 
         block_of_users = (z_lo + later) & 1
         accs = [jnp.zeros((8, TILE), F32) for _ in range(2)]
-        for pair in range(NX // 2):
+        for pair in range(2):
             left = jnp.concatenate(
-                [rows[slot, block, 0:BLOCK, :] for block in (2 * pair, 2 * pair + 1)], axis=0
+                [rows[column, first + 2 * pair + block, 0:BLOCK, :] for block in range(2)], axis=0
             )
             here = slice(pair * 2 * BLOCK, (pair + 1) * 2 * BLOCK)
-            weight = jnp.concatenate([spread[slot, here]] * PARTS, axis=1)
+            weight = jnp.concatenate([spread[here]] * PARTS, axis=1)
             for part in range(2):
                 tile = block_of_users * 2 + part
                 scores = jnp.dot(left, users[tile], preferred_element_type=F32)
                 values = jnp.exp2((scores * SCALE).astype(BF16))
-                kernel[slot, tile, here] = values
+                kernel[unit, tile, here] = values
                 weighted = values.astype(F32) * weight
                 accs[part] += jnp.sum(weighted.reshape(2 * BLOCK // 8, 8, TILE), axis=0)
         for part in range(2):
@@ -208,55 +246,63 @@
     column_half[...] = total.reshape(2, 8, 128)
     row_total_ref[...] = column_half[z_lo]
 
-    def sum_columns(slot):
-        for block in range(NX):
+    def sum_columns(unit, column, first):
+        for block in range(4):
             pieces = []
             for half in (0, 1):
                 acc = jnp.zeros((HALF // 8, 8, 128), F32)
                 for tile in range(TILES):
                     for part in range(PARTS):
-                        piece = kernel[slot, tile,
+                        piece = kernel[unit, tile,
                                        block * BLOCK + half * HALF:block * BLOCK + (half + 1) * HALF,
                                        part * 128:(part + 1) * 128]
                         piece = piece.astype(F32).reshape(HALF // 8, 8, 128)
                         acc = acc + piece * user_rows[tile * PARTS + part]
                 pieces.append(acc.reshape(HALF, 128))
             flat = jnp.concatenate(pieces, axis=0).T
-            column_send[slot, block] = jnp.sum(flat, axis=0, keepdims=True)
+            column_send[first + block, column] = jnp.sum(flat, axis=0, keepdims=True)
+
+    def send_columns(slot):
+        hop = (slot + 1) // 2
+        remote(column_send.at[slot], column_y.at[slot], cy_send.at[0], cy_recv.at[0],
+               at_y(NY - hop if slot % 2 else hop)).start()
 
     def column_step(step, carry):
-        slot = step & (NY - 1)
-        sum_columns(slot)
-        hop = (step + 1) >> 1
-        ahead = jnp.where((step & 1) == 0, hop, NY - hop)
-
-        @pl.when(step < NY)
+        column = step & 3
+        late = step < 4
+        unit = jnp.where(
+            late, jnp.where(column == 0, 3, column + 4), jnp.where(column == 3, 4, column)
+        )
+        sum_columns(unit, column, jnp.where(late, 4, 0))
+
+        @pl.when(step == 3)
         def _():
-            remote(column_send.at[slot], column_y.at[slot], cy_send.at[0], cy_recv.at[0],
-                   at_y(ahead)).start()
+            for slot in (7, 5, 6, 4):
+                send_columns(slot)
 
         return carry
 
-    lax.fori_loop(1, NY + 1, column_step, 0)
+    lax.fori_loop(0, 8, column_step, 0)
+    for slot in (3, 1, 2):
+        send_columns(slot)
     column_y[0] = column_send[0]
     settle(column_y.at[1:NY], cy_recv.at[0])
     total = column_y[0]
     for part in range(1, NY):
         total = total + column_y[part]
     column_x[NX] = total
-
-    for step in (1, 3, 2):
-        remote(column_x.at[NX, (x + step) & (NX - 1)], column_x.at[step, 0],
-               cx_send.at[0], cx_recv.at[0], at_x(step)).start()
-    column_x[0, 0] = column_x[NX, x]
+    for column, source, partner in ((3, 3, far), (1, 2, left), (2, 1, right)):
+        remote(column_x.at[NX, column], column_x.at[source, 0],
+               cx_send.at[0], cx_recv.at[0], partner).start()
+    column_x[0, 0] = column_x[NX, 0]
     settle(column_x.at[1:NX, 0], cx_recv.at[0])
     total = column_x[0, 0]
     for part in range(1, NX):
         total = total + column_x[part, 0]
     column_total_ref[...] = total
 
-    settle(rows.at[0, 0:3], x_send.at[0])
-    settle(rows.at[0:7], y_send.at[0])
+    settle(rows.at[0, 1:NY], y_send.at[0])
+    settle(rows.at[1:NX], x_send.at[0])
     for half in (0, 1):
         settle(users.at[half], u_send.at[half])
     settle(masses.at[0], u_send.at[2])
@@ -282,10 +328,10 @@
             pltpu.VMEM((USERS, WIDTH), BF16),
             pltpu.VMEM((BLOCK, WIDTH), BF16),
             pltpu.VMEM((1, BLOCK), BF16),
-            pltpu.VMEM((NY, NX, BLOCK + 16, WIDTH), BF16),
-            pltpu.VMEM((NY, NX * BLOCK, BLOCK), F32),
+            pltpu.VMEM((NX, NY, BLOCK + 16, WIDTH), BF16),
+            pltpu.VMEM((4 * BLOCK, BLOCK), F32),
             pltpu.VMEM((TILES, WIDTH, TILE), BF16),
-            pltpu.VMEM((NY, TILES, NX * BLOCK, TILE), BF16),
+            pltpu.VMEM((NY, TILES, 4 * BLOCK, TILE), BF16),
             pltpu.VMEM((TILES, 8, TILE), F32),
             pltpu.VMEM((LINE, 16, 128), F32),
             pltpu.VMEM((2, 8, 128), F32),
@@ -295,8 +341,9 @@
             pltpu.VMEM((NX + 1, NX, 1, BLOCK), F32),
             pltpu.VMEM((2, 8, 128), F32),
             dma((4,)),
-            dma((1,)), dma((1,)),
-            dma((1,)), dma((2, 5, 2)),
+            dma((1,)), dma((5,)),
+            dma((1,)), dma((5,)),
+            dma((4,)),
             dma((3,)), dma((3,)),
             dma((1,)), dma((1,)),
             dma((1,)), dma((1,)),

time: 56.2 us -> 55.9 us (level); the launches traced: 55.5 us -> 55.7 us
  no operation moved by 1% of the time
where the time goes in v6:
time: 55.9 us; the launch traced here: 55.7 us
  Pallas kernels  53.3 us (95%)
  other arithmetic  1.8 us (3%)
  between operations  0.67 us (1%)
    pallas_call x1, Pallas kernels, on_device(): pl.pallas_call(functools.partial(body, item_count), out_shape=(jax.ShapeD...  53.3 us
    div x1, other arithmetic, on_device(): user_scale = user_mass / (row_total.reshape(1024) / item_count)  1.28 us

profile of v6, /device:TPU:1, one launch (start us, length us, event | category | flops | bytes accessed | tf_op | source)
XLA Modules:
  0.0 55.7 jit_solution(800652654012753210)
XLA Ops:
  0.6 0.0 copy-start
  0.6 53.3 %scaling.1 = (f32[8,128]{1,0:T(8,128)}, f32[1,128]{1,0:T(1,128)}) custom-call(bf16[1024,128]{1,0:T(8,128)(2,1)} %users_hbm.1, bf16[128,128]{1,0:T(8,128)(2,1)} %items_hbm.1, bf16[1,128]{1,0:T(2,128)(2,1)} %bitcast.7, f32[8,128]{1,0:T(8,128)} %bitcast.6), custom_call_target="tpu_custom_call" | custom-call | flops 4294967296 | bytes 1048576 | tf_op jit(solution)/shard_map/scaling/pallas_call | solution.py:319
  53.9 0.0 copy-done
  53.9 0.0 copy-start.1
  53.9 0.0 copy-start.2
  53.9 1.3 %bitcast_divide_fusion = f32[1024]{0:T(1024)} fusion(f32[1024]{0:T(1024)S(1)} %copy-done, f32[8,128]{1,0:T(8,128)} %get-tuple-element.4), kind=kLoop, calls=%fused_computation | loop fusion | flops 2048 | bytes 12288 | tf_op jit(solution)/shard_map/div | solution.py:360
  55.2 0.0 copy-done.1
  55.2 0.0 copy-done.2
  55.2 0.5 bitcast_divide_fusion.1
Async XLA Ops:
  0.6 53.3 %copy-start = (f32[1024]{0:T(1024)S(1)}, f32[1024]{0:T(1024)}, u32[]{:S(2)}) copy-start(f32[1024]{0:T(1024)} %param.8) | copy-start | bytes 12292
  53.9 1.3 %copy-start.1 = (f32[128]{0:T(128)S(1)}, f32[128]{0:T(128)}, u32[]{:S(2)}) copy-start(f32[128]{0:T(128)} %param.9) | copy-start | bytes 1540
  53.9 1.3 %copy-start.2 = (f32[1,128]{1,0:T(1,128)S(1)}, f32[1,128]{1,0:T(1,128)}, u32[]{:S(2)}) copy-start(f32[1,128]{1,0:T(1,128)} %get-tuple-element.5) | copy-start | bytes 1540

commit v7 on v6

--- a/solution.py
+++ b/solution.py
@@ -214,9 +214,9 @@
             for part in range(2):
                 tile = block_of_users * 2 + part
                 scores = jnp.dot(left, users[tile], preferred_element_type=F32)
-                values = jnp.exp2((scores * SCALE).astype(BF16))
+                values = jnp.exp2(scores * SCALE)
                 kernel[unit, tile, here] = values
-                weighted = values.astype(F32) * weight
+                weighted = values * weight
                 accs[part] += jnp.sum(weighted.reshape(2 * BLOCK // 8, 8, TILE), axis=0)
         for part in range(2):
             row_acc[block_of_users * 2 + part] += accs[part]
@@ -256,7 +256,7 @@
                         piece = kernel[unit, tile,
                                        block * BLOCK + half * HALF:block * BLOCK + (half + 1) * HALF,
                                        part * 128:(part + 1) * 128]
-                        piece = piece.astype(F32).reshape(HALF // 8, 8, 128)
+                        piece = piece.reshape(HALF // 8, 8, 128)
                         acc = acc + piece * user_rows[tile * PARTS + part]
                 pieces.append(acc.reshape(HALF, 128))
             flat = jnp.concatenate(pieces, axis=0).T
@@ -331,7 +331,7 @@
             pltpu.VMEM((NX, NY, BLOCK + 16, WIDTH), BF16),
             pltpu.VMEM((4 * BLOCK, BLOCK), F32),
             pltpu.VMEM((TILES, WIDTH, TILE), BF16),
-            pltpu.VMEM((NY, TILES, 4 * BLOCK, TILE), BF16),
+            pltpu.VMEM((NY, TILES, 4 * BLOCK, TILE), F32),
             pltpu.VMEM((TILES, 8, TILE), F32),
             pltpu.VMEM((LINE, 16, 128), F32),
             pltpu.VMEM((2, 8, 128), F32),

time: 55.9 us -> 54 us (0.966)
  Pallas kernels: 53.3 us -> 51.3 us
    pallas_call x1, Pallas kernels: 53.3 us -> 51.3 us  [on_device(): pl.pallas_call(functools.partial(body, item_count), out_shape=(jax.ShapeD...]
where the time goes in v7:
time: 54 us; the launch traced here: 53.8 us
  Pallas kernels  51.3 us (95%)
  other arithmetic  1.8 us (3%)
  between operations  0.67 us (1%)
    pallas_call x1, Pallas kernels, on_device(): pl.pallas_call(functools.partial(body, item_count), out_shape=(jax.ShapeD...  51.3 us
    div x1, other arithmetic, on_device(): user_scale = user_mass / (row_total.reshape(1024) / item_count)  1.28 us

profile of v7, /device:TPU:1, one launch (start us, length us, event | category | flops | bytes accessed | tf_op | source)
XLA Modules:
  0.0 53.8 jit_solution(16079210754143088303)
XLA Ops:
  0.6 0.0 copy-start
  0.6 51.3 %scaling.1 = (f32[8,128]{1,0:T(8,128)}, f32[1,128]{1,0:T(1,128)}) custom-call(bf16[1024,128]{1,0:T(8,128)(2,1)} %users_hbm.1, bf16[128,128]{1,0:T(8,128)(2,1)} %items_hbm.1, bf16[1,128]{1,0:T(2,128)(2,1)} %bitcast.7, f32[8,128]{1,0:T(8,128)} %bitcast.6), custom_call_target="tpu_custom_call" | custom-call | flops 4294967296 | bytes 1048576 | tf_op jit(solution)/shard_map/scaling/pallas_call | solution.py:319
  52.0 0.0 copy-done
  52.0 0.0 copy-start.1
  52.0 0.0 copy-start.2
  52.0 1.3 %bitcast_divide_fusion = f32[1024]{0:T(1024)} fusion(f32[1024]{0:T(1024)S(1)} %copy-done, f32[8,128]{1,0:T(8,128)} %get-tuple-element.4), kind=kLoop, calls=%fused_computation | loop fusion | flops 2048 | bytes 12288 | tf_op jit(solution)/shard_map/div | solution.py:360
  53.3 0.0 copy-done.1
  53.3 0.0 copy-done.2
  53.3 0.5 bitcast_divide_fusion.1
Async XLA Ops:
  0.6 51.3 %copy-start = (f32[1024]{0:T(1024)S(1)}, f32[1024]{0:T(1024)}, u32[]{:S(2)}) copy-start(f32[1024]{0:T(1024)} %param.8) | copy-start | bytes 12292
  52.0 1.3 %copy-start.1 = (f32[128]{0:T(128)S(1)}, f32[128]{0:T(128)}, u32[]{:S(2)}) copy-start(f32[128]{0:T(128)} %param.9) | copy-start | bytes 1540
  52.0 1.3 %copy-start.2 = (f32[1,128]{1,0:T(1,128)S(1)}, f32[1,128]{1,0:T(1,128)}, u32[]{:S(2)}) copy-start(f32[1,128]{1,0:T(1,128)} %get-tuple-element.5) | copy-start | bytes 1540

commit v8 on v7

--- a/solution.py
+++ b/solution.py
@@ -33,7 +33,7 @@
     item_count,
     users_hbm, items_hbm, weight_hbm, mass_hbm,
     row_total_ref, column_total_ref,
-    users_in, items_in, weight_in, rows, spread, users, kernel, row_acc, row_parts, masses,
+    users_in, items_in, weight_in, rows, users, kernel, row_acc, row_parts, masses,
     user_rows, column_send, column_y, column_x, column_half,
     in_sem, x_send, x_recv, y_send, y_recv, f_recv, u_send, u_recv, r_send, r_recv,
     cy_send, cy_recv, cx_send, cx_recv,
@@ -58,21 +58,6 @@
         other = (line + step) & (LINE - 1)
         return (wide_no_z + (((other >> 1) & 1) << 5), ((other >> 2) << 1) | (other & 1))
 
-    barrier = pltpu.get_barrier_semaphore()
-
-    def greet(partner):
-        pl.semaphore_signal(barrier, inc=1, device_id=partner, device_id_type=MESH)
-
-    def greet_line(step, carry):
-        greet(at_line(step))
-        return carry
-
-    for step in (1, 3, 2):
-        greet(at_x(step))
-    for step in (1, 7, 2, 6, 3, 5, 4):
-        greet(at_y(step))
-    lax.fori_loop(1, LINE, greet_line, 0)
-
     get_items = pltpu.make_async_copy(items_hbm, items_in, in_sem.at[0])
     get_weight = pltpu.make_async_copy(weight_hbm, weight_in, in_sem.at[1])
     get_users = pltpu.make_async_copy(users_hbm, users_in, in_sem.at[2])
@@ -81,6 +66,21 @@
     get_weight.start()
     get_users.start()
     get_mass.start()
+
+    barrier = pltpu.get_barrier_semaphore()
+
+    def greet(partner):
+        pl.semaphore_signal(barrier, inc=1, device_id=partner, device_id_type=MESH)
+
+    def greet_line(step, carry):
+        greet(at_line(step))
+        return carry
+
+    for step in (1, 3, 2):
+        greet(at_x(step))
+    for step in (1, 7, 2, 6, 3, 5, 4):
+        greet(at_y(step))
+    lax.fori_loop(1, LINE, greet_line, 0)
 
     get_items.wait()
     get_weight.wait()
@@ -162,10 +162,9 @@
         column = jnp.where(unit < 3, unit, jnp.where(unit == 3, 0, jnp.where(unit == 4, 3, unit - 4)))
         return column, jnp.where(late, 4, 0)
 
-    def spread_weights(column, first):
-        for block in range(4):
-            weight = rows[column, first + block, BLOCK:BLOCK + 16, :].astype(F32)[0:1]
-            spread[block * BLOCK:(block + 1) * BLOCK] = jnp.broadcast_to(weight, (BLOCK, BLOCK)).T
+    def spread_weight(column, slot):
+        weight = rows[column, slot, BLOCK:BLOCK + 16, :].astype(F32)[0:1]
+        return jnp.broadcast_to(weight, (BLOCK, BLOCK)).T
 
     def before(at):
         if at == 2:
@@ -193,10 +192,6 @@
             def _():
                 before(known)
 
-        @pl.when(later == 0)
-        def _():
-            spread_weights(column, first)
-
         @pl.when(at == 1)
         def _():
             for half in (0, 1):
@@ -206,14 +201,14 @@
         block_of_users = (z_lo + later) & 1
         accs = [jnp.zeros((8, TILE), F32) for _ in range(2)]
         for pair in range(2):
-            left = jnp.concatenate(
-                [rows[column, first + 2 * pair + block, 0:BLOCK, :] for block in range(2)], axis=0
-            )
+            both = [first + 2 * pair, first + 2 * pair + 1]
+            left_rows = jnp.concatenate([rows[column, slot, 0:BLOCK, :] for slot in both], axis=0)
             here = slice(pair * 2 * BLOCK, (pair + 1) * 2 * BLOCK)
-            weight = jnp.concatenate([spread[here]] * PARTS, axis=1)
+            weight = jnp.concatenate([spread_weight(column, slot) for slot in both], axis=0)
+            weight = jnp.concatenate([weight] * PARTS, axis=1)
             for part in range(2):
                 tile = block_of_users * 2 + part
-                scores = jnp.dot(left, users[tile], preferred_element_type=F32)
+                scores = jnp.dot(left_rows, users[tile], preferred_element_type=F32)
                 values = jnp.exp2(scores * SCALE)
                 kernel[unit, tile, here] = values
                 weighted = values * weight
@@ -260,45 +255,34 @@
                         acc = acc + piece * user_rows[tile * PARTS + part]
                 pieces.append(acc.reshape(HALF, 128))
             flat = jnp.concatenate(pieces, axis=0).T
-            column_send[first + block, column] = jnp.sum(flat, axis=0, keepdims=True)
-
-    def send_columns(slot):
-        hop = (slot + 1) // 2
-        remote(column_send.at[slot], column_y.at[slot], cy_send.at[0], cy_recv.at[0],
-               at_y(NY - hop if slot % 2 else hop)).start()
+            column_send[column, first + block] = jnp.sum(flat, axis=0, keepdims=True)
 
     def column_step(step, carry):
-        column = step & 3
-        late = step < 4
+        turn, late = step >> 1, (step & 1) == 1
+        column = jnp.where(turn == 0, 3, jnp.where(turn == 3, 0, turn))
         unit = jnp.where(
             late, jnp.where(column == 0, 3, column + 4), jnp.where(column == 3, 4, column)
         )
         sum_columns(unit, column, jnp.where(late, 4, 0))
-
-        @pl.when(step == 3)
-        def _():
-            for slot in (7, 5, 6, 4):
-                send_columns(slot)
+        for known, done, source, partner in ((1, 3, 3, far), (3, 1, 2, left), (5, 2, 1, right)):
+            @pl.when(step == known)
+            def _():
+                remote(column_send.at[done], column_x.at[source],
+                       cx_send.at[0], cx_recv.at[0], partner).start()
 
         return carry
 
     lax.fori_loop(0, 8, column_step, 0)
-    for slot in (3, 1, 2):
-        send_columns(slot)
-    column_y[0] = column_send[0]
+    settle(column_x.at[1:NX], cx_recv.at[0])
+    column_x[0] = column_send[0] + column_x[1] + column_x[2] + column_x[3]
+    for slot in (7, 5, 6, 3, 4, 1, 2):
+        hop = (slot + 1) // 2
+        remote(column_x.at[0, slot], column_y.at[slot], cy_send.at[0], cy_recv.at[0],
+               at_y(NY - hop if slot % 2 else hop)).start()
     settle(column_y.at[1:NY], cy_recv.at[0])
-    total = column_y[0]
+    total = column_x[0, 0]
     for part in range(1, NY):
         total = total + column_y[part]
-    column_x[NX] = total
-    for column, source, partner in ((3, 3, far), (1, 2, left), (2, 1, right)):
-        remote(column_x.at[NX, column], column_x.at[source, 0],
-               cx_send.at[0], cx_recv.at[0], partner).start()
-    column_x[0, 0] = column_x[NX, 0]
-    settle(column_x.at[1:NX, 0], cx_recv.at[0])
-    total = column_x[0, 0]
-    for part in range(1, NX):
-        total = total + column_x[part, 0]
     column_total_ref[...] = total
 
     settle(rows.at[0, 1:NY], y_send.at[0])
@@ -308,7 +292,7 @@
     settle(masses.at[0], u_send.at[2])
     settle(row_parts.at[0:LINE - 1], r_send.at[0])
     settle(column_y.at[1:NY], cy_send.at[0])
-    settle(column_x.at[1:NX, 0], cx_send.at[0])
+    settle(column_x.at[1:NX], cx_send.at[0])
 
 
 def on_device(users, items, item_scale, user_mass, item_mass):
@@ -329,16 +313,15 @@
             pltpu.VMEM((BLOCK, WIDTH), BF16),
             pltpu.VMEM((1, BLOCK), BF16),
             pltpu.VMEM((NX, NY, BLOCK + 16, WIDTH), BF16),
-            pltpu.VMEM((4 * BLOCK, BLOCK), F32),
             pltpu.VMEM((TILES, WIDTH, TILE), BF16),
             pltpu.VMEM((NY, TILES, 4 * BLOCK, TILE), F32),
             pltpu.VMEM((TILES, 8, TILE), F32),
             pltpu.VMEM((LINE, 16, 128), F32),
             pltpu.VMEM((2, 8, 128), F32),
             pltpu.VMEM((TILES * PARTS, 8, 128), F32),
-            pltpu.VMEM((NY, NX, 1, BLOCK), F32),
-            pltpu.VMEM((NY, NX, 1, BLOCK), F32),
-            pltpu.VMEM((NX + 1, NX, 1, BLOCK), F32),
+            pltpu.VMEM((NX, NY, 1, BLOCK), F32),
+            pltpu.VMEM((NY, 1, BLOCK), F32),
+            pltpu.VMEM((NX, NY, 1, BLOCK), F32),
             pltpu.VMEM((2, 8, 128), F32),
             dma((4,)),
             dma((1,)), dma((5,)),

time: 54 us -> 52.6 us (0.974)
  Pallas kernels: 51.3 us -> 49.5 us
    pallas_call x1, Pallas kernels: 51.3 us -> 49.5 us  [on_device(): pl.pallas_call(functools.partial(body, item_count), out_shape=(jax.ShapeD...]
where the time goes in v8:
time: 52.6 us; the launch traced here: 51.9 us
  Pallas kernels  49.5 us (94%)
  other arithmetic  1.8 us (3%)
  between operations  0.67 us (1%)
    pallas_call x1, Pallas kernels, on_device(): pl.pallas_call(functools.partial(body, item_count), out_shape=(jax.ShapeD...  49.5 us
    div x1, other arithmetic, on_device(): user_scale = user_mass / (row_total.reshape(1024) / item_count)  1.28 us

profile of v8, /device:TPU:1, one launch (start us, length us, event | category | flops | bytes accessed | tf_op | source)
XLA Modules:
  0.0 51.9 jit_solution(3112079269006694908)
XLA Ops:
  0.6 0.0 copy-start
  0.6 49.5 %scaling.1 = (f32[8,128]{1,0:T(8,128)}, f32[1,128]{1,0:T(1,128)}) custom-call(bf16[1024,128]{1,0:T(8,128)(2,1)} %users_hbm.1, bf16[128,128]{1,0:T(8,128)(2,1)} %items_hbm.1, bf16[1,128]{1,0:T(2,128)(2,1)} %bitcast.7, f32[8,128]{1,0:T(8,128)} %bitcast.6), custom_call_target="tpu_custom_call" | custom-call | flops 4294967296 | bytes 1048576 | tf_op jit(solution)/shard_map/scaling/pallas_call | solution.py:303
  50.1 0.0 copy-done
  50.1 0.0 copy-start.1
  50.1 0.0 copy-start.2
  50.1 1.3 %bitcast_divide_fusion = f32[1024]{0:T(1024)} fusion(f32[1024]{0:T(1024)S(1)} %copy-done, f32[8,128]{1,0:T(8,128)} %get-tuple-element.4), kind=kLoop, calls=%fused_computation | loop fusion | flops 2048 | bytes 12288 | tf_op jit(solution)/shard_map/div | solution.py:343
  51.4 0.0 copy-done.1
  51.4 0.0 copy-done.2
  51.4 0.5 %bitcast_divide_fusion.1 = f32[128]{0:T(128)} fusion(f32[128]{0:T(128)S(1)} %copy-done.1, f32[1,128]{1,0:T(1,128)S(1)} %copy-done.2), kind=kLoop, calls=%fused_computation.1 | loop fusion | flops 256 | bytes 1536 | tf_op jit(solution)/shard_map/div | solution.py:344
Async XLA Ops:
  0.6 49.5 %copy-start = (f32[1024]{0:T(1024)S(1)}, f32[1024]{0:T(1024)}, u32[]{:S(2)}) copy-start(f32[1024]{0:T(1024)} %param.8) | copy-start | bytes 12292
  50.1 1.3 %copy-start.1 = (f32[128]{0:T(128)S(1)}, f32[128]{0:T(128)}, u32[]{:S(2)}) copy-start(f32[128]{0:T(128)} %param.9) | copy-start | bytes 1540
  50.1 1.3 %copy-start.2 = (f32[1,128]{1,0:T(1,128)S(1)}, f32[1,128]{1,0:T(1,128)}, u32[]{:S(2)}) copy-start(f32[1,128]{1,0:T(1,128)} %get-tuple-element.5) | copy-start | bytes 1540

commit v9 on v8

--- a/solution.py
+++ b/solution.py
@@ -199,22 +199,24 @@
             settle(masses.at[0], u_recv.at[2])
 
         block_of_users = (z_lo + later) & 1
-        accs = [jnp.zeros((8, TILE), F32) for _ in range(2)]
-        for pair in range(2):
-            both = [first + 2 * pair, first + 2 * pair + 1]
-            left_rows = jnp.concatenate([rows[column, slot, 0:BLOCK, :] for slot in both], axis=0)
-            here = slice(pair * 2 * BLOCK, (pair + 1) * 2 * BLOCK)
-            weight = jnp.concatenate([spread_weight(column, slot) for slot in both], axis=0)
-            weight = jnp.concatenate([weight] * PARTS, axis=1)
-            for part in range(2):
-                tile = block_of_users * 2 + part
-                scores = jnp.dot(left_rows, users[tile], preferred_element_type=F32)
+        wide_of = TILE // 2
+        accs = [jnp.zeros((8, wide_of), F32) for _ in range(4)]
+        for block in range(4):
+            left_rows = rows[column, first + block, 0:BLOCK, :]
+            weight = spread_weight(column, first + block)
+            weight = jnp.concatenate([weight] * (wide_of // 128), axis=1)
+            here = slice(block * BLOCK, (block + 1) * BLOCK)
+            for part in range(4):
+                tile = block_of_users * 2 + part // 2
+                there = slice(part % 2 * wide_of, (part % 2 + 1) * wide_of)
+                scores = jnp.dot(left_rows, users[tile, :, there], preferred_element_type=F32)
                 values = jnp.exp2(scores * SCALE)
-                kernel[unit, tile, here] = values
-                weighted = values * weight
-                accs[part] += jnp.sum(weighted.reshape(2 * BLOCK // 8, 8, TILE), axis=0)
-        for part in range(2):
-            row_acc[block_of_users * 2 + part] += accs[part]
+                kernel[unit, tile, here, there] = values
+                weighted = (values * weight).reshape(BLOCK // 8, 8, wide_of)
+                accs[part] += jnp.sum(weighted, axis=0)
+        for part in range(4):
+            there = slice(part % 2 * wide_of, (part % 2 + 1) * wide_of)
+            row_acc[block_of_users * 2 + part // 2, :, there] += accs[part]
         return carry
 
     lax.fori_loop(0, 16, compute_step, 0)
@@ -303,8 +305,8 @@
     row_total, column_total = pl.pallas_call(
         functools.partial(body, item_count),
         out_shape=(
-            jax.ShapeDtypeStruct((8, 128), F32),
-            jax.ShapeDtypeStruct((1, 128), F32),
+            pltpu.VMEM((8, 128), F32),
+            pltpu.VMEM((1, 128), F32),
         ),
         in_specs=[pl.BlockSpec(memory_space=pl.ANY)] * 4,
         out_specs=(vmem, vmem),

time: 52.6 us -> 51.4 us (0.977)
  other arithmetic: 1.8 us -> 1.12 us
  Pallas kernels: 49.5 us -> 48.9 us
    div x1, other arithmetic: 1.28 us -> 0.6 us  [on_device(): user_scale = user_mass / (row_total.reshape(1024) / item_count)]
    pallas_call x1, Pallas kernels: 49.5 us -> 48.9 us  [on_device(): pl.pallas_call(functools.partial(body, item_count), out_shape=(pltpu.VMEM...]
where the time goes in v9:
time: 51.4 us; the launch traced here: 50.7 us
  Pallas kernels  48.9 us (95%)
  other arithmetic  1.12 us (2%)
  between operations  0.66 us (1%)
    pallas_call x1, Pallas kernels, on_device(): pl.pallas_call(functools.partial(body, item_count), out_shape=(pltpu.VMEM...  48.9 us

profile of v9, /device:TPU:1, one launch (start us, length us, event | category | flops | bytes accessed | tf_op | source)
XLA Modules:
  0.0 50.7 jit_solution(18020146120748893200)
XLA Ops:
  0.6 0.0 copy-start
  0.6 48.9 %scaling.1 = (f32[8,128]{1,0:T(8,128)S(1)}, f32[1,128]{1,0:T(1,128)S(1)}) custom-call(bf16[1024,128]{1,0:T(8,128)(2,1)} %users_hbm.1, bf16[128,128]{1,0:T(8,128)(2,1)} %items_hbm.1, bf16[1,128]{1,0:T(2,128)(2,1)} %bitcast.7, f32[8,128]{1,0:T(8,128)} %bitcast.6), custom_call_target="tpu_custom_call" | custom-call | flops 4294967296 | bytes 1048576 | tf_op jit(solution)/shard_map/scaling/pallas_call | solution.py:305
  49.5 0.0 copy-done
  49.5 0.0 copy-start.1
  49.5 0.6 %bitcast_divide_fusion = f32[1024]{0:T(1024)} fusion(f32[1024]{0:T(1024)S(1)} %copy-done, f32[8,128]{1,0:T(8,128)S(1)} %get-tuple-element.4), kind=kLoop, calls=%fused_computation | loop fusion | flops 2048 | bytes 12288 | tf_op jit(solution)/shard_map/div | solution.py:345
  50.1 0.0 copy-done.1
  50.2 0.5 %bitcast_divide_fusion.1 = f32[128]{0:T(128)} fusion(f32[128]{0:T(128)S(1)} %copy-done.1, f32[1,128]{1,0:T(1,128)S(1)} %get-tuple-element.5), kind=kLoop, calls=%fused_computation.1 | loop fusion | flops 256 | bytes 1536 | tf_op jit(solution)/shard_map/div | solution.py:346
Async XLA Ops:
  0.6 48.9 %copy-start = (f32[1024]{0:T(1024)S(1)}, f32[1024]{0:T(1024)}, u32[]{:S(2)}) copy-start(f32[1024]{0:T(1024)} %param.8) | copy-start | bytes 12292
  49.5 0.7 %copy-start.1 = (f32[128]{0:T(128)S(1)}, f32[128]{0:T(128)}, u32[]{:S(2)}) copy-start(f32[128]{0:T(128)} %param.9) | copy-start | bytes 1540

commit v10 on v9

--- a/solution.py
+++ b/solution.py
@@ -146,7 +146,7 @@
     get_users.wait()
     get_mass.wait()
     for half, partner in ((0, up), (1, down)):
-        values = users_in[half * TILE:(half + 1) * TILE, :].astype(F32).T
+        values = users_in[half * TILE:(half + 1) * TILE, :].T.astype(F32)
         tile = z_lo * 2 + half
         users[tile] = unit_rows(values, 0)
         part = users.at[tile]
@@ -163,8 +163,8 @@
         return column, jnp.where(late, 4, 0)
 
     def spread_weight(column, slot):
-        weight = rows[column, slot, BLOCK:BLOCK + 16, :].astype(F32)[0:1]
-        return jnp.broadcast_to(weight, (BLOCK, BLOCK)).T
+        weight = rows[column, slot, BLOCK:BLOCK + 16, :]
+        return jnp.concatenate([weight] * (BLOCK // 16), axis=0).T.astype(F32)
 
     def before(at):
         if at == 2:

time: 51.4 us -> 51.3 us (level)
  no operation moved by 1% of the time
where the time goes in v10:
time: 51.3 us; the launch traced here: 50.7 us
  Pallas kernels  48.8 us (95%)
  other arithmetic  1.12 us (2%)
  between operations  0.66 us (1%)
    pallas_call x1, Pallas kernels, on_device(): pl.pallas_call(functools.partial(body, item_count), out_shape=(pltpu.VMEM...  48.8 us

profile of v10, /device:TPU:1, one launch (start us, length us, event | category | flops | bytes accessed | tf_op | source)
XLA Modules:
  0.0 50.7 jit_solution(4850947436011003455)
XLA Ops:
  0.6 0.0 copy-start
  0.6 48.8 %scaling.1 = (f32[8,128]{1,0:T(8,128)S(1)}, f32[1,128]{1,0:T(1,128)S(1)}) custom-call(bf16[1024,128]{1,0:T(8,128)(2,1)} %users_hbm.1, bf16[128,128]{1,0:T(8,128)(2,1)} %items_hbm.1, bf16[1,128]{1,0:T(2,128)(2,1)} %bitcast.7, f32[8,128]{1,0:T(8,128)} %bitcast.6), custom_call_target="tpu_custom_call" | custom-call | flops 4294967296 | bytes 1048576 | tf_op jit(solution)/shard_map/scaling/pallas_call | solution.py:305
  49.5 0.0 copy-done
  49.5 0.0 copy-start.1
  49.5 0.6 %bitcast_divide_fusion = f32[1024]{0:T(1024)} fusion(f32[1024]{0:T(1024)S(1)} %copy-done, f32[8,128]{1,0:T(8,128)S(1)} %get-tuple-element.4), kind=kLoop, calls=%fused_computation | loop fusion | flops 2048 | bytes 12288 | tf_op jit(solution)/shard_map/div | solution.py:345
  50.1 0.0 copy-done.1
  50.1 0.5 %bitcast_divide_fusion.1 = f32[128]{0:T(128)} fusion(f32[128]{0:T(128)S(1)} %copy-done.1, f32[1,128]{1,0:T(1,128)S(1)} %get-tuple-element.5), kind=kLoop, calls=%fused_computation.1 | loop fusion | flops 256 | bytes 1536 | tf_op jit(solution)/shard_map/div | solution.py:346
Async XLA Ops:
  0.6 48.8 %copy-start = (f32[1024]{0:T(1024)S(1)}, f32[1024]{0:T(1024)}, u32[]{:S(2)}) copy-start(f32[1024]{0:T(1024)} %param.8) | copy-start | bytes 12292
  49.5 0.7 %copy-start.1 = (f32[128]{0:T(128)S(1)}, f32[128]{0:T(128)}, u32[]{:S(2)}) copy-start(f32[128]{0:T(128)} %param.9) | copy-start | bytes 1540

commit v11 on v10

--- a/solution.py
+++ b/solution.py
@@ -139,8 +139,6 @@
     y_send_to(1)
     x_send_of(0)
     y_send_to(2)
-    y_send_to(3)
-    y_send_to(4)
 
     up, down = at_line(2), at_line(LINE - 2)
     get_users.wait()
@@ -154,6 +152,8 @@
     remote(masses.at[z_lo], masses.at[z_lo], u_send.at[2], u_recv.at[2], up).start()
 
     from_y(1)
+    y_send_to(3)
+    y_send_to(4)
     from_y(2)
     row_acc[...] = jnp.zeros_like(row_acc)
 
@@ -168,10 +168,11 @@
 
     def before(at):
         if at == 2:
-            from_y(3)
             from_x(0)
             from_x(1)
             from_x(2)
+        elif at == 3:
+            from_y(3)
         elif at == 5:
             from_y(4)
         elif at == 6:
@@ -187,7 +188,7 @@
     def compute_step(at, carry):
         unit, later = at >> 1, at & 1
         column, first = unit_of(unit)
-        for known in (2, 5, 6, 8, 10, 14):
+        for known in (2, 3, 5, 6, 8, 10, 14):
             @pl.when(at == known)
             def _():
                 before(known)

time: 51.3 us -> 51.2 us (level)
  no operation moved by 1% of the time
where the time goes in v11:
time: 51.2 us; the launch traced here: 50.5 us
  Pallas kernels  48.7 us (95%)
  other arithmetic  1.12 us (2%)
  between operations  0.66 us (1%)
    pallas_call x1, Pallas kernels, on_device(): pl.pallas_call(functools.partial(body, item_count), out_shape=(pltpu.VMEM...  48.7 us

profile of v11, /device:TPU:1, one launch (start us, length us, event | category | flops | bytes accessed | tf_op | source)
XLA Modules:
  0.0 50.5 jit_solution(11532227450219522499)
XLA Ops:
  0.6 0.0 copy-start
  0.6 48.7 %scaling.1 = (f32[8,128]{1,0:T(8,128)S(1)}, f32[1,128]{1,0:T(1,128)S(1)}) custom-call(bf16[1024,128]{1,0:T(8,128)(2,1)} %users_hbm.1, bf16[128,128]{1,0:T(8,128)(2,1)} %items_hbm.1, bf16[1,128]{1,0:T(2,128)(2,1)} %bitcast.7, f32[8,128]{1,0:T(8,128)} %bitcast.6), custom_call_target="tpu_custom_call" | custom-call | flops 4294967296 | bytes 1048576 | tf_op jit(solution)/shard_map/scaling/pallas_call | solution.py:306
  49.3 0.0 copy-done
  49.4 0.0 copy-start.1
  49.4 0.6 %bitcast_divide_fusion = f32[1024]{0:T(1024)} fusion(f32[1024]{0:T(1024)S(1)} %copy-done, f32[8,128]{1,0:T(8,128)S(1)} %get-tuple-element.4), kind=kLoop, calls=%fused_computation | loop fusion | flops 2048 | bytes 12288 | tf_op jit(solution)/shard_map/div | solution.py:346
  50.0 0.0 copy-done.1
  50.0 0.5 %bitcast_divide_fusion.1 = f32[128]{0:T(128)} fusion(f32[128]{0:T(128)S(1)} %copy-done.1, f32[1,128]{1,0:T(1,128)S(1)} %get-tuple-element.5), kind=kLoop, calls=%fused_computation.1 | loop fusion | flops 256 | bytes 1536 | tf_op jit(solution)/shard_map/div | solution.py:347
Async XLA Ops:
  0.6 48.7 %copy-start = (f32[1024]{0:T(1024)S(1)}, f32[1024]{0:T(1024)}, u32[]{:S(2)}) copy-start(f32[1024]{0:T(1024)} %param.8) | copy-start | bytes 12292
  49.4 0.7 %copy-start.1 = (f32[128]{0:T(128)S(1)}, f32[128]{0:T(128)}, u32[]{:S(2)}) copy-start(f32[128]{0:T(128)} %param.9) | copy-start | bytes 1540

commit v12 on v11

--- a/solution.py
+++ b/solution.py
@@ -15,7 +15,6 @@
 NX, NY, NZ = 4, 8, 8
 LINE = 2 * NZ
 BLOCK = 128
-HALF = 64
 USERS = 1024
 TILE = 512
 TILES = 2 * USERS // TILE
@@ -228,12 +227,14 @@
             at = tile * PARTS + part
             row_parts[line, at:at + 1, :] = total[:, part * 128:(part + 1) * 128]
 
-    def send_rows(step, carry):
+    def send_rows(turn, carry):
+        off = (turn + 1) >> 1
+        step = jnp.where((turn & 1) == 1, NZ - off, NZ + off)
         remote(row_parts.at[line], row_parts.at[line], r_send.at[0], r_recv.at[0],
                at_line(step)).start()
         return carry
 
-    lax.fori_loop(1, LINE, send_rows, 0)
+    lax.fori_loop(0, LINE - 1, send_rows, 0)
     settle(row_parts.at[0:LINE - 1], r_recv.at[0])
     total = row_parts[0]
     for part in range(1, LINE):
@@ -246,18 +247,13 @@
 
     def sum_columns(unit, column, first):
         for block in range(4):
-            pieces = []
-            for half in (0, 1):
-                acc = jnp.zeros((HALF // 8, 8, 128), F32)
-                for tile in range(TILES):
-                    for part in range(PARTS):
-                        piece = kernel[unit, tile,
-                                       block * BLOCK + half * HALF:block * BLOCK + (half + 1) * HALF,
-                                       part * 128:(part + 1) * 128]
-                        piece = piece.reshape(HALF // 8, 8, 128)
-                        acc = acc + piece * user_rows[tile * PARTS + part]
-                pieces.append(acc.reshape(HALF, 128))
-            flat = jnp.concatenate(pieces, axis=0).T
+            acc = jnp.zeros((BLOCK // 8, 8, 128), F32)
+            for tile in range(TILES):
+                for part in range(PARTS):
+                    piece = kernel[unit, tile, block * BLOCK:(block + 1) * BLOCK,
+                                   part * 128:(part + 1) * 128]
+                    acc = acc + piece.reshape(BLOCK // 8, 8, 128) * user_rows[tile * PARTS + part]
+            flat = acc.reshape(BLOCK, 128).T
             column_send[column, first + block] = jnp.sum(flat, axis=0, keepdims=True)
 
     def column_step(step, carry):

time: 51.2 us -> 51.1 us (level)
  no operation moved by 1% of the time
where the time goes in v12:
time: 51.1 us; the launch traced here: 50.4 us
  Pallas kernels  48.6 us (95%)
  other arithmetic  1.12 us (2%)
  between operations  0.66 us (1%)
    pallas_call x1, Pallas kernels, on_device(): pl.pallas_call(functools.partial(body, item_count), out_shape=(pltpu.VMEM...  48.6 us

profile of v12, /device:TPU:1, one launch (start us, length us, event | category | flops | bytes accessed | tf_op | source)
XLA Modules:
  0.0 50.4 jit_solution(4934909766153630374)
XLA Ops:
  0.6 0.0 copy-start
  0.6 48.6 %scaling.1 = (f32[8,128]{1,0:T(8,128)S(1)}, f32[1,128]{1,0:T(1,128)S(1)}) custom-call(bf16[1024,128]{1,0:T(8,128)(2,1)} %users_hbm.1, bf16[128,128]{1,0:T(8,128)(2,1)} %items_hbm.1, bf16[1,128]{1,0:T(2,128)(2,1)} %bitcast.7, f32[8,128]{1,0:T(8,128)} %bitcast.6), custom_call_target="tpu_custom_call" | custom-call | flops 4294967296 | bytes 1048576 | tf_op jit(solution)/shard_map/scaling/pallas_call | solution.py:302
  49.3 0.0 copy-done
  49.3 0.0 copy-start.1
  49.3 0.6 %bitcast_divide_fusion = f32[1024]{0:T(1024)} fusion(f32[1024]{0:T(1024)S(1)} %copy-done, f32[8,128]{1,0:T(8,128)S(1)} %get-tuple-element.4), kind=kLoop, calls=%fused_computation | loop fusion | flops 2048 | bytes 12288 | tf_op jit(solution)/shard_map/div | solution.py:342
  49.9 0.0 copy-done.1
  49.9 0.5 %bitcast_divide_fusion.1 = f32[128]{0:T(128)} fusion(f32[128]{0:T(128)S(1)} %copy-done.1, f32[1,128]{1,0:T(1,128)S(1)} %get-tuple-element.5), kind=kLoop, calls=%fused_computation.1 | loop fusion | flops 256 | bytes 1536 | tf_op jit(solution)/shard_map/div | solution.py:343
Async XLA Ops:
  0.6 48.6 %copy-start = (f32[1024]{0:T(1024)S(1)}, f32[1024]{0:T(1024)}, u32[]{:S(2)}) copy-start(f32[1024]{0:T(1024)} %param.8) | copy-start | bytes 12292
  49.3 0.7 %copy-start.1 = (f32[128]{0:T(128)S(1)}, f32[128]{0:T(128)}, u32[]{:S(2)}) copy-start(f32[128]{0:T(128)} %param.9) | copy-start | bytes 1540
